TPU v7x, 32 devices: a whole 2x2x4 slice. The times are simulated.
32 devices in a mesh: section: 4 (over y, x), seq: 2 (over core), dp: 4 (over z).
Axes of the slice: x: 2, y: 2, z: 4, core: 2. Of those that a mesh axis runs over, the one named last changes fastest.
Arguments:
- bases: int32 [8, 3072, 128], P('dp', 'seq'), may hold values from 0 to 3
- targets: int32 [8, 3072, 4096], P('dp', 'seq', 'section'), may hold values from 0 to 2
- stem_weight: bfloat16 [512, 384], replicated, may hold values from -0.5 to 0.5
- conv_weight: bfloat16 [4, 3, 384, 192], P('section'), may hold values from -0.1875 to 0.1875
- proj_weight: bfloat16 [4, 192, 384], P('section'), may hold values from -0.4375 to 0.4375
- head_weight: bfloat16 [384, 4096], P(None, 'section'), may hold values from -0.078125 to 0.078125
Outputs:
- conv_grad: float32 [4, 3, 384, 192], P('section')
- proj_grad: float32 [4, 192, 384], P('section')
- head_grad: float32 [384, 4096], P(None, 'section')
All inputs are finite; a program needn't handle non-finite values.
Results may differ from a plain program's by a relative error of at most 0.0014.
Values may be sent and summed in bfloat16 or wider, within the bound.
A program may use at most 128 MiB of HBM per device.

v0:
```python
import math

import jax
import jax.numpy as jnp
from jax import lax
from jax.experimental import pallas as pl
from jax.experimental.pallas import tpu as pltpu
from jax.sharding import PartitionSpec as P

SQRT_TWO_OVER_PI = 0.7978845608028654
CUBIC_TERM = 0.044715


def gelu_value(inputs):
    return (
        0.5
        * inputs
        * (1.0 + jnp.tanh(SQRT_TWO_OVER_PI * (inputs + CUBIC_TERM * inputs * inputs * inputs)))
    )


def gelu_slope(inputs):
    tangent = jnp.tanh(SQRT_TWO_OVER_PI * (inputs + CUBIC_TERM * inputs * inputs * inputs))
    return 0.5 * (1.0 + tangent) + 0.5 * inputs * (1.0 - tangent * tangent) * SQRT_TWO_OVER_PI * (
        1.0 + 3.0 * CUBIC_TERM * inputs * inputs
    )


def contract_rows(left_side, right_side):
    return lax.dot_general(
        left_side, right_side, (((0,), (0,)), ((), ())), preferred_element_type=jnp.float32
    )


def times_transposed(left_side, right_side):
    return lax.dot_general(
        left_side, right_side, (((1,), (1,)), ((), ())), preferred_element_type=jnp.float32
    )


def shift_rows(value, by):
    if abs(by) >= value.shape[0]:
        return jnp.zeros_like(value)
    pad = jnp.zeros((abs(by),) + value.shape[1:], value.dtype)
    if by > 0:
        return jnp.concatenate([pad, value[:-by]], 0)
    return jnp.concatenate([value[-by:], pad], 0)


MESH = pl.DeviceIdType.MESH
ANY = pl.BlockSpec(memory_space=pl.ANY)


def greet(peers):
    barrier = pltpu.get_barrier_semaphore()
    for peer in peers:
        pl.semaphore_signal(barrier, inc=1, device_id=peer, device_id_type=MESH)
    pl.semaphore_wait(barrier, len(peers))


def remote(src, dst, send, recv, peer):
    return pltpu.make_async_remote_copy(
        src_ref=src, dst_ref=dst, send_sem=send, recv_sem=recv, device_id=peer, device_id_type=MESH
    )


def gather_weights(conv, proj, sections):
    def kernel(conv_ref, proj_ref, conv_out, proj_out, send, recv, local, send2, recv2):
        s, c = lax.axis_index("section"), lax.axis_index("seq")
        others = [lax.rem(s + k, sections) for k in range(1, sections)]
        partner = {"section": s, "seq": 1 - c}
        peers = [{"section": o, "seq": c} for o in others]
        greet(peers + [partner])
        pairs = ((conv_ref, conv_out), (proj_ref, proj_out))
        first, second, own = [], [], []
        for k, peer in enumerate(peers):
            for n, (src, out) in enumerate(pairs):
                first.append(remote(src.at[c], out.at[s, c], send.at[k, n], recv.at[k, n], peer))
                first[-1].start()
        for n, (src, out) in enumerate(pairs):
            own.append(pltpu.make_async_copy(src, out.at[s], local.at[n]))
            own[-1].start()
        for k in range(sections - 1):
            source = lax.rem(s + sections - 1 - k, sections)
            for n, (_, out) in enumerate(pairs):
                first[2 * k + n].wait_recv()
                piece = out.at[source, c]
                second.append(remote(piece, piece, send2.at[k, n], recv2.at[k, n], partner))
                second[-1].start()
        for copy in second:
            copy.wait()
        for copy in first:
            copy.wait_send()
        for copy in own:
            copy.wait()

    sems = pltpu.SemaphoreType.DMA((sections - 1, 2))
    return pl.pallas_call(
        kernel,
        out_shape=[
            jax.ShapeDtypeStruct((sections,) + conv.shape, conv.dtype),
            jax.ShapeDtypeStruct((sections,) + proj.shape, proj.dtype),
        ],
        in_specs=[ANY] * 2,
        out_specs=[ANY] * 2,
        scratch_shapes=[sems, sems, pltpu.SemaphoreType.DMA((2,)), sems, sems],
        compiler_params=pltpu.CompilerParams(collective_id=0, has_side_effects=True),
    )(conv, proj)


def exchange(value, sections, seqs, columns, to_head):
    group = sections * seqs

    def kernel(src, out, send, recv, local):
        s, c = lax.axis_index("section"), lax.axis_index("seq")
        me = s * seqs + c

        def part(ref, batch, section):
            start = pl.multiple_of(section * columns, 16)
            return ref.at[batch, :, pl.ds(start, columns), :]

        def ends(ps, pc):
            if to_head:
                return src.at[pc], part(out, c, s)
            return part(src, pc, ps), out.at[s, c]

        places = []
        for k in range(1, group):
            p = lax.rem(me + k, group)
            places.append((p // seqs, lax.rem(p, seqs)))
        peers = [{"section": ps, "seq": pc} for ps, pc in places]
        greet(peers)
        copies = []
        for k, (ps, pc) in enumerate(places):
            source, target = ends(ps, pc)
            copies.append(remote(source, target, send.at[k], recv.at[k], peers[k]))
            copies[-1].start()
        source, target = ends(s, c)
        own = pltpu.make_async_copy(source, target, local)
        own.start()
        own.wait()
        for copy in copies:
            copy.wait()

    q, channels = value.shape[1], value.shape[3]
    if to_head:
        shape = (seqs, q, sections * columns, channels)
    else:
        shape = (sections, seqs, q, columns, channels)
    sems = pltpu.SemaphoreType.DMA((group - 1,))
    return pl.pallas_call(
        kernel,
        out_shape=jax.ShapeDtypeStruct(shape, value.dtype),
        in_specs=[pl.BlockSpec(memory_space=pltpu.VMEM)],
        out_specs=pl.BlockSpec(memory_space=pltpu.VMEM),
        scratch_shapes=[sems, sems, pltpu.SemaphoreType.DMA],
        compiler_params=pltpu.CompilerParams(
            collective_id=1 if to_head else 2, has_side_effects=True, vmem_limit_bytes=16 * 2**20
        ),
    )(value)


def sum_gradients(value, sections, zones):
    rows, width = value.shape[1:]
    half = rows // 2
    piece = half // zones

    def kernel(
        src, out, met, wire, came, total, zcame, s0, r0, s1, r1, s2, r2, s3, r3, s4, r4
    ):
        s, c, d = (lax.axis_index(name) for name in ("section", "seq", "dp"))
        partner = {"section": s, "seq": 1 - c, "dp": d}
        order = [lax.rem(s + k, sections) for k in range(1, sections + 1)]
        across = [{"section": o, "seq": c, "dp": d} for o in order[:-1]]
        levels = [lax.rem(d + k, zones) for k in range(1, zones)]
        along = [{"section": s, "seq": c, "dp": z} for z in levels]
        greet([partner] + across + along)

        def strip(z):
            return pl.ds(pl.multiple_of(z * piece, 8), piece)

        def far(o):
            return src.at[o, pl.ds(pl.multiple_of((1 - c) * half, 8), half), :]

        def near(o):
            return src[o, pl.ds(pl.multiple_of(c * half, 8), half), :]

        pair = [remote(far(o), met.at[k], s0.at[k], r0.at[k], partner) for k, o in enumerate(order)]
        for copy in pair:
            copy.start()
        hops = []
        for k, peer in enumerate(across):
            pair[k].wait_recv()
            wire[k] = (met[k] + near(order[k])).astype(wire.dtype)
            hops.append(remote(wire.at[k], came.at[k], s1.at[k], r1.at[k], peer))
            hops[-1].start()
        pair[sections - 1].wait_recv()
        total[...] = met[sections - 1] + near(order[sections - 1])
        for k, copy in enumerate(hops):
            copy.wait_recv()
            total[...] += came[k].astype(jnp.float32)
        climbs = []
        for k, peer in enumerate(along):
            climbs.append(
                remote(total.at[strip(levels[k])], zcame.at[k], s2.at[k], r2.at[k], peer)
            )
            climbs[-1].start()
        done = total[strip(d), :]
        for k, copy in enumerate(climbs):
            copy.wait_recv()
            done = done + zcame[k]
        out[c, strip(d), :] = done

        mine = out.at[c, strip(d)]
        backs = [remote(mine, mine, s3.at[k], r3.at[k], peer) for k, peer in enumerate(along)]
        for copy in backs:
            copy.start()
        ends = [remote(mine, mine, s4.at[0], r4.at[0], partner)]
        ends[0].start()
        for k in range(zones - 1):
            backs[k].wait_recv()
            landed = out.at[c, strip(lax.rem(d + zones - 1 - k, zones))]
            ends.append(remote(landed, landed, s4.at[k + 1], r4.at[k + 1], partner))
            ends[-1].start()
        for copy in ends:
            copy.wait()
        for copy in pair + hops + climbs + backs:
            copy.wait_send()

    def dma(count):
        return [pltpu.SemaphoreType.DMA((count,))] * 2

    out = pl.pallas_call(
        kernel,
        out_shape=jax.ShapeDtypeStruct((2, half, width), jnp.float32),
        in_specs=[pl.BlockSpec(memory_space=pltpu.VMEM)],
        out_specs=pl.BlockSpec(memory_space=pltpu.VMEM),
        scratch_shapes=[
            pltpu.VMEM((sections, half, width), jnp.float32),
            pltpu.VMEM((sections - 1, half, width), jnp.bfloat16),
            pltpu.VMEM((sections - 1, half, width), jnp.bfloat16),
            pltpu.VMEM((half, width), jnp.float32),
            pltpu.VMEM((zones - 1, piece, width), jnp.float32),
        ]
        + dma(sections) + dma(sections - 1) + dma(zones - 1) + dma(zones - 1) + dma(zones),
        compiler_params=pltpu.CompilerParams(
            collective_id=3, has_side_effects=True, vmem_limit_bytes=40 * 2**20
        ),
    )(value)
    return out.reshape(rows, width)


def body(bases, targets, stem_weight, conv_weight, proj_weight, head_weight):
    sections = lax.axis_size("section")
    seqs = lax.axis_size("seq")
    section_number = lax.axis_index("section")
    batches, row_count, bin_width = bases.shape
    channels = stem_weight.shape[1]
    length = row_count * seqs
    factor = 1.0 / math.sqrt(batches * lax.axis_size("dp") * length)
    unit = length // 2**sections
    local_q = row_count // unit
    blocks = length // unit
    columns = batches * unit // (seqs * sections)

    paired = seqs == 2 and batches == seqs and columns % 16 == 0

    if paired:
        conv_all, proj_all = gather_weights(
            conv_weight.reshape(2, -1, conv_weight.shape[-1]),
            proj_weight.reshape(2, -1, channels),
            sections,
        )
        conv_all = conv_all.reshape((sections,) + conv_weight.shape[1:])
        proj_all = proj_all.reshape((sections,) + proj_weight.shape[1:])
    else:
        conv_all = lax.all_gather(conv_weight, "section", axis=0, tiled=True)
        proj_all = lax.all_gather(proj_weight, "section", axis=0, tiled=True)

    def to_chains(value):
        value = lax.all_to_all(value, "seq", split_axis=1, concat_axis=0, tiled=True)
        return value.reshape(blocks * columns, value.shape[-1])

    own = bases.reshape(batches, local_q, unit, bin_width).transpose(1, 0, 2, 3)
    own = own.reshape(local_q, seqs, sections, columns, bin_width)
    own = lax.dynamic_index_in_dim(own, section_number, 2, keepdims=False)
    picked = to_chains(own.astype(jnp.bfloat16))
    onehot = jnp.concatenate([(picked == c).astype(jnp.bfloat16) for c in range(4)], 1)
    stem = stem_weight.reshape(bin_width, 4, channels).transpose(1, 0, 2).reshape(-1, channels)
    state = jnp.dot(onehot, stem, preferred_element_type=jnp.float32).astype(jnp.bfloat16)

    saved = []
    for layer in range(sections):
        by = columns * 2**layer
        taps = conv_all[layer].reshape(-1, conv_all.shape[-1])
        hidden = gelu_value(state.astype(jnp.float32)).astype(jnp.bfloat16)
        wide = jnp.concatenate([shift_rows(hidden, by), hidden, shift_rows(hidden, -by)], 1)
        inner_sum = jnp.dot(wide, taps, preferred_element_type=jnp.float32)
        active = gelu_value(inner_sum).astype(jnp.bfloat16)
        update = jnp.dot(active, proj_all[layer], preferred_element_type=jnp.float32)
        saved.append((state, wide, inner_sum, active))
        state = (state.astype(jnp.float32) + update).astype(jnp.bfloat16)

    lifted = gelu_value(state.astype(jnp.float32)).astype(jnp.bfloat16)
    if paired:
        lifted = lifted.reshape(seqs, local_q, columns, channels)
        lifted = exchange(lifted, sections, seqs, columns, True)
    else:
        lifted = lifted.reshape(seqs, local_q, 1, columns, channels)
        lifted = lax.all_to_all(lifted, "seq", split_axis=0, concat_axis=2, tiled=True)
        lifted = lifted.reshape(local_q, seqs, 1, columns, channels)
        lifted = lax.all_gather(lifted, "section", axis=2, tiled=True)
        lifted = lifted.reshape(local_q, batches, unit, channels).transpose(1, 0, 2, 3)
    lifted = lifted.reshape(batches * row_count, channels)

    logits = jnp.dot(lifted, head_weight, preferred_element_type=jnp.float32)
    counts = targets.reshape(batches * row_count, targets.shape[2]).astype(jnp.float32)
    slope = ((jnp.exp(logits) - counts) * factor).astype(jnp.bfloat16)
    head_sum = lax.psum(contract_rows(lifted, slope), ("seq", "dp"))
    lift_part = times_transposed(slope, head_weight)

    if paired:
        lift_part = lift_part.astype(jnp.bfloat16).reshape(batches, local_q, unit, channels)
        terms = exchange(lift_part, sections, seqs, columns, False)
        lift_grad = terms.astype(jnp.float32).sum(0).reshape(blocks * columns, channels)
    else:
        lift_part = lift_part.reshape(batches, local_q, unit, channels).transpose(1, 0, 2, 3)
        lift_part = lift_part.reshape(local_q, seqs, sections, columns, channels)
        lift_part = lax.psum_scatter(lift_part, "section", scatter_dimension=2, tiled=True)
        lift_grad = to_chains(lift_part.reshape(local_q, seqs, columns, channels))

    grad = (lift_grad * gelu_slope(state.astype(jnp.float32))).astype(jnp.bfloat16)
    parts = []
    for layer in reversed(range(sections)):
        by = columns * 2**layer
        start_state, wide, inner_sum, active = saved[layer]
        kernel = conv_all[layer]
        proj_part = contract_rows(active, grad)
        active_grad = times_transposed(grad, proj_all[layer])
        inner_grad = (active_grad * gelu_slope(inner_sum)).astype(jnp.bfloat16)
        parts.append(jnp.concatenate([contract_rows(inner_grad, wide), proj_part], 1))
        wide_grad = jnp.concatenate(
            [shift_rows(inner_grad, -by), inner_grad, shift_rows(inner_grad, by)], 1
        )
        turned = kernel.transpose(0, 2, 1).reshape(-1, channels)
        hidden_grad = jnp.dot(wide_grad, turned, preferred_element_type=jnp.float32)
        grad = (
            grad.astype(jnp.float32) + hidden_grad * gelu_slope(start_state.astype(jnp.float32))
        ).astype(jnp.bfloat16)
    parts = jnp.stack(parts[::-1])
    zones = lax.axis_size("dp")
    if paired and zones > 1 and parts.shape[1] % (16 * zones) == 0:
        total = sum_gradients(parts, sections, zones)
    else:
        total = lax.psum_scatter(parts, "section", scatter_dimension=0, tiled=True)
        total = lax.psum(total[0], ("seq", "dp"))
    taps_width = total.shape[1] - channels
    conv_sum = total[:, :taps_width].T.reshape(conv_weight.shape)
    return conv_sum, total[:, taps_width:][None], head_sum


def solution(mesh):
    in_specs = (
        P("dp", "seq", None),
        P("dp", "seq", "section"),
        P(),
        P("section", None, None, None),
        P("section", None, None),
        P(None, "section"),
    )
    out_specs = (P("section", None, None, None), P("section", None, None), P(None, "section"))
    return jax.shard_map(body, mesh=mesh, in_specs=in_specs, out_specs=out_specs, check_vma=False)
```

profile of v0, /device:TPU:0, one launch (start us, length us, event | category | flops | bytes accessed | tf_op | source)
XLA Modules:
  0.0 223.3 jit_solution(7485576537706653296)
XLA Ops:
  7.2 1.8 fusion.157
  9.0 3.4 %all-to-all-start = ((bf16[8,2,48,128]{3,2,0,1:T(8,128)(2,1)}), bf16[8,2,48,128]{3,2,0,1:T(8,128)(2,1)S(1)}, u32[]{:S(2)}, u32[]{:S(2)}) async-start(bf16[8,2,48,128]{3,2,0,1:T(8,128)(2,1)} %fusion.157), calls=%async_computation | async-start | bytes 393216 | tf_op jit(solution)/shard_map/all_to_all | solution.py:281
  12.7 1.1 copy.16
  14.2 1.6 fusion.76
  15.9 27.6 %shard_map.85 = (bf16[4,2,576,192]{3,2,1,0:T(8,128)(2,1)}, bf16[4,2,96,384]{3,2,1,0:T(8,128)(2,1)}) custom-call(bf16[2,576,192]{2,1,0:T(8,128)(2,1)} %bitcast.124, bf16[2,96,384]{2,1,0:T(8,128)(2,1)} %bitcast.139), custom_call_target="tpu_custom_call" | custom-call | tf_op jit(solution)/shard_map/pallas_call | solution.py:98
  43.6 1.8 fusion.207
  45.6 0.8 fusion.201
  46.4 0.7 copy-done.56
  47.1 0.7 fusion.65
  48.1 0.8 fusion.216
  48.9 0.7 fusion.61
  49.8 0.7 fusion.164
  51.1 0.7 fusion.57
  51.9 0.7 fusion.160
  53.0 1.5 fusion.69
  54.6 26.5 %shard_map.86 = bf16[2,8,192,384]{3,2,1,0:T(8,128)(2,1)S(1)} custom-call(bf16[2,8,48,384]{3,2,1,0:T(8,128)(2,1)S(1)} %bitcast.117), custom_call_target="tpu_custom_call" | custom-call | tf_op jit(solution)/shard_map/pallas_call | solution.py:151
  81.1 7.2 %fusion.1 = bf16[3072,1024]{1,0:T(8,128)(2,1)S(1)} fusion(bf16[3072,384]{1,0:T(8,128)(2,1)S(1)} %bitcast.112, bf16[384,1024]{1,0:T(8,128)(2,1)S(1)} %copy-done, s32[2,1536,1024]{2,1,0:T(8,128)} %param.7), kind=kOutput, calls=%fused_computation.2 | convolution fusion | flops 2428502016 | bytes 22020096 | tf_op jit(solution)/shard_map/dot_general | solution.py:316
  88.4 2.6 %copy-done.2 = bf16[3072,1024]{1,0:T(8,128)(2,1)} copy-done((bf16[3072,1024]{1,0:T(8,128)(2,1)}, bf16[3072,1024]{1,0:T(8,128)(2,1)S(1)}, u32[]{:S(2)}) %copy-start.2) | copy-done | bytes 6291480
  91.0 3.8 %fusion.218 = f32[384,1024]{1,0:T(8,128)} fusion(bf16[3072,384]{1,0:T(8,128)(2,1)S(1)} %bitcast.113, bf16[3072,1024]{1,0:T(8,128)(2,1)S(1)} %fusion.1), kind=kOutput, calls=%fused_computation.277 | convolution fusion | flops 2415919104 | bytes 10223616 | tf_op jit(solution)/shard_map/dot_general | solution.py:30
  94.8 6.3 %convolution_convert_fusion = bf16[3072,384]{1,0:T(8,128)(2,1)S(1)} fusion(bf16[3072,1024]{1,0:T(8,128)(2,1)} %copy-done.2, bf16[384,1024]{1,0:T(8,128)(2,1)S(1)} %copy-done), kind=kOutput, calls=%fused_computation.5 | convolution fusion | flops 2417098752 | bytes 9437184 | tf_op jit(solution)/shard_map/dot_general | solution.py:36
  101.0 28.9 %shard_map.87 = bf16[4,2,8,48,384]{4,3,2,1,0:T(8,128)(2,1)S(1)} custom-call(bf16[2,8,192,384]{3,2,1,0:T(8,128)(2,1)S(1)} %bitcast.116), custom_call_target="tpu_custom_call" | custom-call | tf_op jit(solution)/shard_map/pallas_call | solution.py:151
  130.3 0.7 copy-done.19
  131.0 0.8 fusion.74
  132.2 0.5 fusion.53
  133.0 1.1 fusion.206
  134.3 1.5 fusion.158
  135.8 0.7 fusion.215
  136.5 1.0 copy.17
  137.5 2.9 %fusion.43 = bf16[768,384]{1,0:T(8,128)(2,1)S(1)} fusion(bf16[576,384]{1,0:T(8,128)(2,1)} %bitcast.127, bf16[768,384]{1,0:T(8,128)(2,1)} %copy-done.55, bf16[768,384]{1,0:T(8,128)(2,1)} %copy-done.20, bf16[384,192]{0,1:T(8,128)(2,1)} %get-tuple-element.34, bf16[384,192]{0,1:T(8,128)(2,1)S(1)} %get-tuple-element.33, bf16[768,192]{0,1:T(8,128)(2,1)S(1)} %fusion.53), kind=kOutput, calls=%fused_computation.91 | convolution fusion | flops 350650368 | bytes 2801664 | tf_op jit(solution)/shard_map/dot_general | solution.py:346
  140.4 0.5 fusion.54
  141.2 1.1 fusion.205
  142.6 1.5 fusion.162
  144.1 0.9 fusion.214
  145.4 1.0 copy.18
  146.4 3.1 %fusion.44 = bf16[768,384]{1,0:T(8,128)(2,1)S(1)} fusion(bf16[576,384]{1,0:T(8,128)(2,1)} %bitcast.128, bf16[768,384]{1,0:T(8,128)(2,1)} %copy-done.54, bf16[768,384]{1,0:T(8,128)(2,1)} %copy-done.51, bf16[576,192]{0,1:T(8,128)(2,1)} %get-tuple-element.32, bf16[576,192]{0,1:T(8,128)(2,1)} %get-tuple-element.31, bf16[768,192]{0,1:T(8,128)(2,1)S(1)} %fusion.54), kind=kOutput, calls=%fused_computation.92 | convolution fusion | flops 350650368 | bytes 2949120 | tf_op jit(solution)/shard_map/dot_general | solution.py:346
  149.5 0.5 fusion.55
  150.3 1.1 fusion.204
  151.4 1.5 fusion.217
  153.4 3.8 %fusion.45 = bf16[768,384]{1,0:T(8,128)(2,1)} fusion(bf16[576,384]{1,0:T(8,128)(2,1)S(1)} %bitcast.129, bf16[768,384]{1,0:T(8,128)(2,1)} %copy-done.53, bf16[768,384]{1,0:T(8,128)(2,1)} %copy-done.52, bf16[672,192]{0,1:T(8,128)(2,1)S(1)} %get-tuple-element.30, bf16[672,192]{0,1:T(8,128)(2,1)S(1)} %get-tuple-element.29, bf16[768,192]{0,1:T(8,128)(2,1)S(1)} %fusion.55), kind=kOutput, calls=%fused_computation.93 | convolution fusion | flops 350650368 | bytes 3022848 | tf_op jit(solution)/shard_map/dot_general | solution.py:346
  157.2 2.3 %fusion.92 = f32[192,1152]{1,0:T(8,128)S(1)} fusion(bf16[768,384]{1,0:T(8,128)(2,1)} %fusion.45, bf16[192,384]{1,0:T(8,128)(2,1)S(1)} %bitcast.132, f32[768,192]{0,1:T(8,128)} %copy-done.46, bf16[720,384]{1,0:T(8,128)(2,1)S(1)} %copy-done.24, bf16[720,384]{1,0:T(8,128)(2,1)S(1)} %copy-done.22, bf16[768,384]{1,0:T(8,128)(2,1)S(1)} %copy-done.9), kind=kOutput, calls=%fused_computation.146 | convolution fusion | flops 464633856 | bytes 3907584 | tf_op jit(solution)/shard_map/dot_general | solution.py:30
  159.5 1.7 fusion.203
  161.6 0.9 copy-done.3
  163.1 46.4 %shard_map.88 = f32[2,96,1536]{2,1,0:T(8,128)S(1)} custom-call(f32[4,192,1536]{2,1,0:T(8,128)S(1)} %pad_maximum_fusion.src), custom_call_target="tpu_custom_call" | custom-call | tf_op jit(solution)/shard_map/pallas_call | solution.py:233
  209.6 1.0 slice_bitcast_fusion
  210.6 1.5 reshape.123
  212.0 1.0 copy.20
  213.0 0.7 slice_bitcast_fusion.1
  213.8 2.7 %copy.22 = f32[384,1024]{1,0:T(8,128)} copy(f32[384,1024]{1,0:T(8,128)} %all-reduce.16.cloned.1.call-done) | data formatting | bytes 3145728
  (129 shorter events, 6.3 us)
Async XLA Ops:
  7.2 74.0 %copy-start = (bf16[384,1024]{1,0:T(8,128)(2,1)S(1)}, bf16[384,1024]{1,0:T(8,128)(2,1)}, u32[]{:S(2)}) copy-start(bf16[384,1024]{1,0:T(8,128)(2,1)} %param.11) | copy-start | bytes 2359300
  7.2 5.3 %copy-start.30 = (bf16[512,384]{1,0:T(8,128)(2,1)S(1)}, bf16[512,384]{1,0:T(8,128)(2,1)}, u32[]{:S(2)}) copy-start(bf16[512,384]{1,0:T(8,128)(2,1)} %param.8) | copy-start | bytes 1179652
  7.2 5.5 %copy-start.29 = (bf16[1,3,384,192]{2,3,1,0:T(8,128)(2,1)S(1)}, bf16[1,3,384,192]{2,3,1,0:T(8,128)(2,1)}, u32[]{:S(2)}) copy-start(bf16[1,3,384,192]{2,3,1,0:T(8,128)(2,1)} %param.9) | copy-start | bytes 1327108
  9.0 4.9 %all-to-all-start = ((bf16[8,2,48,128]{3,2,0,1:T(8,128)(2,1)}), bf16[8,2,48,128]{3,2,0,1:T(8,128)(2,1)S(1)}, u32[]{:S(2)}, u32[]{:S(2)}) async-start(bf16[8,2,48,128]{3,2,0,1:T(8,128)(2,1)} %fusion.157), calls=%async_computation | async-start | bytes 393216 | tf_op jit(solution)/shard_map/all_to_all | solution.py:281
  12.5 201.3 %all-reduce.16.cloned.1.call-start = ((), (), s32[]{:S(2)}) async-start(), calls=%async_computation.1 | async-start | bytes 3145728 | tf_op jit(solution)/shard_map/psum | solution.py:319
  15.8 29.7 %copy-start.8 = (bf16[768,384]{1,0:T(8,128)(2,1)}, bf16[768,384]{1,0:T(8,128)(2,1)S(1)}, u32[]{:S(2)}) copy-start(bf16[768,384]{1,0:T(8,128)(2,1)S(1)} %get-tuple-element.39) | copy-start | bytes 1769476
  15.9 29.6 %copy-start.21 = (bf16[720,384]{1,0:T(8,128)(2,1)}, bf16[720,384]{1,0:T(8,128)(2,1)S(1)}, u32[]{:S(2)}) copy-start(bf16[720,384]{1,0:T(8,128)(2,1)S(1)} %get-tuple-element.23) | copy-start | bytes 1658884
  15.9 29.6 %copy-start.23 = (bf16[720,384]{1,0:T(8,128)(2,1)}, bf16[720,384]{1,0:T(8,128)(2,1)S(1)}, u32[]{:S(2)}) copy-start(bf16[720,384]{1,0:T(8,128)(2,1)S(1)} %get-tuple-element.24) | copy-start | bytes 1658884
  43.6 1.9 copy-start.16
  45.4 4.4 %copy-start.4 = (bf16[1,2,576,192]{3,2,1,0:T(8,128)(2,1)}, bf16[1,2,576,192]{3,2,1,0:T(8,128)(2,1)S(1)}, u32[]{:S(2)}) copy-start(bf16[1,2,576,192]{3,2,1,0:T(8,128)(2,1)S(1)} %get-tuple-element.14) | copy-start | bytes 1327108
  45.4 6.5 %copy-start.6 = (bf16[1,2,576,192]{3,2,1,0:T(8,128)(2,1)}, bf16[1,2,576,192]{3,2,1,0:T(8,128)(2,1)S(1)}, u32[]{:S(2)}) copy-start(bf16[1,2,576,192]{3,2,1,0:T(8,128)(2,1)S(1)} %get-tuple-element.13) | copy-start | bytes 1327108
  45.5 3.3 %copy-start.40 = (bf16[1,2,96,384]{3,2,1,0:T(8,128)(2,1)}, bf16[1,2,96,384]{3,2,1,0:T(8,128)(2,1)S(1)}, u32[]{:S(2)}) copy-start(bf16[1,2,96,384]{3,2,1,0:T(8,128)(2,1)S(1)} %get-tuple-element.28) | copy-start | bytes 442372
  45.5 5.3 %copy-start.42 = (bf16[1,2,96,384]{3,2,1,0:T(8,128)(2,1)}, bf16[1,2,96,384]{3,2,1,0:T(8,128)(2,1)S(1)}, u32[]{:S(2)}) copy-start(bf16[1,2,96,384]{3,2,1,0:T(8,128)(2,1)S(1)} %get-tuple-element.27) | copy-start | bytes 442372
  45.5 7.3 %copy-start.44 = (bf16[1,2,96,384]{3,2,1,0:T(8,128)(2,1)}, bf16[1,2,96,384]{3,2,1,0:T(8,128)(2,1)S(1)}, u32[]{:S(2)}) copy-start(bf16[1,2,96,384]{3,2,1,0:T(8,128)(2,1)S(1)} %get-tuple-element.26) | copy-start | bytes 442372
  45.6 1.5 copy-start.56
  46.3 1.5 copy-start.46
  47.8 1.0 copy-start.53
  49.7 1.4 copy-start.54
  49.8 1.1 copy-start.27
  51.8 1.2 copy-start.55
  51.9 1.0 copy-start.36
  52.8 1.7 copy-start.49
  88.4 2.6 %copy-start.2 = (bf16[3072,1024]{1,0:T(8,128)(2,1)}, bf16[3072,1024]{1,0:T(8,128)(2,1)S(1)}, u32[]{:S(2)}) copy-start(bf16[3072,1024]{1,0:T(8,128)(2,1)S(1)} %fusion.1) | copy-start | bytes 18874372
  129.9 1.1 copy-start.19
  131.0 1.2 copy-start.50
  133.0 1.1 copy-start.15
  133.0 1.2 copy-start.35
  133.0 1.3 copy-start.37
  134.3 2.2 copy-start.7
  137.5 2.9 %copy-start.43 = (bf16[1,2,96,384]{3,2,1,0:T(8,128)(2,1)S(1)}, bf16[1,2,96,384]{3,2,1,0:T(8,128)(2,1)}, u32[]{:S(2)}) copy-start(bf16[1,2,96,384]{3,2,1,0:T(8,128)(2,1)} %copy-done.42) | copy-start | bytes 442372
  137.5 2.9 %copy-start.48 = (f32[768,192]{0,1:T(8,128)S(1)}, f32[768,192]{0,1:T(8,128)}, u32[]{:S(2)}) copy-start(f32[768,192]{0,1:T(8,128)} %copy-done.47) | copy-start | bytes 1769476
  141.2 1.1 copy-start.11
  141.2 1.2 copy-start.26
  141.2 1.4 copy-start.28
  144.1 1.2 copy-start.5
  146.4 3.1 %copy-start.18 = (f32[768,192]{0,1:T(8,128)S(1)}, f32[768,192]{0,1:T(8,128)}, u32[]{:S(2)}) copy-start(f32[768,192]{0,1:T(8,128)} %copy-done.17) | copy-start | bytes 1769476
  146.4 3.1 %copy-start.41 = (bf16[1,2,96,384]{3,2,1,0:T(8,128)(2,1)S(1)}, bf16[1,2,96,384]{3,2,1,0:T(8,128)(2,1)}, u32[]{:S(2)}) copy-start(bf16[1,2,96,384]{3,2,1,0:T(8,128)(2,1)} %copy-done.40) | copy-start | bytes 442372
  153.3 3.8 %copy-start.9 = (bf16[768,384]{1,0:T(8,128)(2,1)S(1)}, bf16[768,384]{1,0:T(8,128)(2,1)}, u32[]{:S(2)}) copy-start(bf16[768,384]{1,0:T(8,128)(2,1)} %copy-done.8) | copy-start | bytes 1769476
  153.3 3.8 %copy-start.22 = (bf16[720,384]{1,0:T(8,128)(2,1)S(1)}, bf16[720,384]{1,0:T(8,128)(2,1)}, u32[]{:S(2)}) copy-start(bf16[720,384]{1,0:T(8,128)(2,1)} %copy-done.21) | copy-start | bytes 1658884
  153.4 3.8 %copy-start.24 = (bf16[720,384]{1,0:T(8,128)(2,1)S(1)}, bf16[720,384]{1,0:T(8,128)(2,1)}, u32[]{:S(2)}) copy-start(bf16[720,384]{1,0:T(8,128)(2,1)} %copy-done.23) | copy-start | bytes 1658884
  153.4 3.8 %copy-start.39 = (bf16[1,2,96,384]{3,2,1,0:T(8,128)(2,1)S(1)}, bf16[1,2,96,384]{3,2,1,0:T(8,128)(2,1)}, u32[]{:S(2)}) copy-start(bf16[1,2,96,384]{3,2,1,0:T(8,128)(2,1)} %copy-done.38) | copy-start | bytes 442372
  157.2 4.1 %copy-start.31 = (f32[192,384]{1,0:T(8,128)S(1)}, f32[192,384]{1,0:T(8,128)}, u32[]{:S(2)}) copy-start(f32[192,384]{1,0:T(8,128)} %fusion.206) | copy-start | bytes 884740
  157.2 4.1 %copy-start.32 = (f32[192,384]{1,0:T(8,128)S(1)}, f32[192,384]{1,0:T(8,128)}, u32[]{:S(2)}) copy-start(f32[192,384]{1,0:T(8,128)} %fusion.205) | copy-start | bytes 884740
  159.5 1.8 copy-start.12
  159.5 1.8 copy-start.13
  161.3 1.2 copy-start.3
  161.3 1.2 copy-start.33
  213.0 3.5 %copy-start.1 = (bf16[384,1024]{1,0:T(8,128)(2,1)S(1)}, bf16[384,1024]{1,0:T(8,128)(2,1)}, u32[]{:S(2)}) copy-start(bf16[384,1024]{1,0:T(8,128)(2,1)} %param.11) | copy-start | bytes 2359300
  (11 other events, 9.5 us)
Sparse Core Ops, SparseCore 0:
  94.9 63.7 all-reduce.15
where the time goes:
time: 225 us; the launch traced here: 223 us
  Pallas kernels  130 us (58%)
  matrix products  48.5 us (22%)
  local copies, waits for them, and re-layouts  22.5 us (10%)
  between operations  14.8 us (7%)
  other arithmetic  4.32 us (2%)
  starting transfers between devices  3.47 us (2%)
    pallas_call x2, Pallas kernels, exchange(): pl.pallas_call(kernel, out_shape=jax.ShapeDtypeStruct(shape, value.dtype)...  55.5 us
    pallas_call x1, Pallas kernels, sum_gradients(): pl.pallas_call(kernel, out_shape=jax.ShapeDtypeStruct((2, half, width), j...  46.4 us
    pallas_call x1, Pallas kernels, gather_weights(): pl.pallas_call(kernel, out_shape=[jax.ShapeDtypeStruct((sections,) + conv...  27.6 us
    dot_general x9, matrix products, contract_rows(): lax.dot_general(left_side, right_side, (((0,), (0,)), ((), ())), preferre...  15.5 us
    unnamed x117, local copies, waits for them, and re-layouts  13 us
    dot_general x3, matrix products, body(): hidden_grad = jnp.dot(wide_grad, turned, preferred_element_type=jnp.float32)  9.76 us
    dot_general x4, matrix products, times_transposed(): lax.dot_general(left_side, right_side, (((1,), (1,)), ((), ())), preferre...  7.83 us
    dot_general x1, matrix products, body(): logits = jnp.dot(lifted, head_weight, preferred_element_type=jnp.float32)  7.23 us
  transfers between devices with their start and end apart: 2, of which 1 were waited for; matrix products, arithmetic and copies ran while one was open for 18% of the time, Pallas kernels for 34%

commit v1 on v0

--- a/solution.py
+++ b/solution.py
@@ -64,100 +64,411 @@
     )
 
 
-def gather_weights(conv, proj, sections):
-    def kernel(conv_ref, proj_ref, conv_out, proj_out, send, recv, local, send2, recv2):
+def both_gelu(inputs):
+    square = inputs * inputs
+    tangent = jnp.tanh(
+        inputs * (SQRT_TWO_OVER_PI + (SQRT_TWO_OVER_PI * CUBIC_TERM) * square)
+    )
+    gate = 0.5 + 0.5 * tangent
+    value = inputs * gate
+    inside = 2.0 * SQRT_TWO_OVER_PI + (6.0 * SQRT_TWO_OVER_PI * CUBIC_TERM) * square
+    return value, gate + value * (1.0 - gate) * inside
+
+
+def tile_of(rows):
+    for size in (512, 384, 256, 192, 128, 96, 64, 48, 32, 16):
+        if rows % size == 0:
+            return size
+    return rows
+
+
+def forward_tower(bases, stem, taps, proj, sections, unit):
+    seqs, half, width = bases.shape
+    length = seqs * half
+    channels = stem.shape[1]
+    inner = proj.shape[0]
+    rows = taps.shape[0] + inner
+    part = rows // 2
+    tile = tile_of(half)
+    steps = half // tile
+    shifts = [unit * 2**k for k in range(sections)]
+
+    def kernel(*refs):
+        bases_ref, stem_ref, taps_ref, proj_ref = refs[:4]
+        refs = refs[4:]
+        top_ref, weights_ref = refs[:2]
+        hidden_out, slope_out = refs[2 : 2 + sections], refs[2 + sections : 1 + 2 * sections]
+        refs = refs[1 + 2 * sections :]
+        active_out, bend_out = refs[:sections], refs[sections : 2 * sections]
+        refs = refs[2 * sections :]
+        full, held, turned, state = refs[:4]
+        refs = refs[4:]
+        hidden, slope = refs[:sections], refs[sections : 2 * sections - 1]
+        refs = refs[2 * sections - 1 :]
+        active, bend = refs[:sections], refs[sections : 2 * sections]
+        refs = refs[2 * sections :]
+        bsend, brecv, send, recv, send2, recv2, tsend, trecv, own_sem, out_sem = refs
+
         s, c = lax.axis_index("section"), lax.axis_index("seq")
-        others = [lax.rem(s + k, sections) for k in range(1, sections)]
         partner = {"section": s, "seq": 1 - c}
-        peers = [{"section": o, "seq": c} for o in others]
+        peers = [{"section": lax.rem(s + k, sections), "seq": c} for k in range(1, sections)]
+        loads = [
+            pltpu.make_async_copy(bases_ref.at[c], full.at[c], own_sem.at[0]),
+            pltpu.make_async_copy(
+                taps_ref, held.at[s, pl.ds(0, taps.shape[0])], own_sem.at[1]
+            ),
+            pltpu.make_async_copy(
+                proj_ref, held.at[s, pl.ds(taps.shape[0], inner)], own_sem.at[2]
+            ),
+        ]
+        for copy in loads:
+            copy.start()
         greet(peers + [partner])
-        pairs = ((conv_ref, conv_out), (proj_ref, proj_out))
-        first, second, own = [], [], []
+        across = remote(bases_ref.at[1 - c], full.at[c], bsend, brecv, partner)
+        across.start()
+        loads[1].wait()
+        loads[2].wait()
+        mine = held.at[s, pl.ds(pl.multiple_of(c * part, 16), part)]
+        first = []
         for k, peer in enumerate(peers):
-            for n, (src, out) in enumerate(pairs):
-                first.append(remote(src.at[c], out.at[s, c], send.at[k, n], recv.at[k, n], peer))
-                first[-1].start()
-        for n, (src, out) in enumerate(pairs):
-            own.append(pltpu.make_async_copy(src, out.at[s], local.at[n]))
-            own[-1].start()
+            first.append(remote(mine, mine, send.at[k], recv.at[k], peer))
+            first[-1].start()
+        for k in range(sections):
+            edge = jnp.zeros((shifts[k], channels), jnp.bfloat16)
+            hidden[k][pl.ds(0, shifts[k]), :] = edge
+            hidden[k][pl.ds(shifts[k] + length, shifts[k]), :] = edge
+
+        def begin(number):
+            def step(i, carry):
+                at = i * tile
+                codes = full[number, pl.ds(pl.multiple_of(at, 16), tile), :]
+                onehot = jnp.concatenate(
+                    [(codes == k).astype(jnp.bfloat16) for k in range(4)], 1
+                )
+                start = jnp.dot(onehot, stem_ref[...], preferred_element_type=jnp.float32)
+                start = start.astype(jnp.bfloat16)
+                place = pl.multiple_of(number * half + at, 16)
+                state[pl.ds(place, tile), :] = start
+                value = gelu_value(start.astype(jnp.float32)).astype(jnp.bfloat16)
+                hidden[0][pl.ds(pl.multiple_of(shifts[0] + place, 16), tile), :] = value
+                return carry
+
+            lax.fori_loop(0, steps, step, 0)
+
+        loads[0].wait()
+        begin(c)
+        across.wait_recv()
+        begin(1 - c)
+
+        second = []
         for k in range(sections - 1):
+            first[k].wait_recv()
             source = lax.rem(s + sections - 1 - k, sections)
-            for n, (_, out) in enumerate(pairs):
-                first[2 * k + n].wait_recv()
-                piece = out.at[source, c]
-                second.append(remote(piece, piece, send2.at[k, n], recv2.at[k, n], partner))
-                second[-1].start()
+            piece = held.at[source, pl.ds(pl.multiple_of(c * part, 16), part)]
+            second.append(remote(piece, piece, send2.at[k], recv2.at[k], partner))
+            second[-1].start()
         for copy in second:
+            copy.wait_recv()
+
+        outs = []
+
+        def keep(src, dst):
+            outs.append(pltpu.make_async_copy(src, dst, out_sem.at[len(outs)]))
+            outs[-1].start()
+
+        keep(held, weights_ref)
+        keep(hidden[0].at[pl.ds(shifts[0], length)], hidden_out[0])
+
+        for k in range(sections):
+            by = shifts[k]
+            for j in range(3):
+                tap = held[k, pl.ds(j * inner, inner), :]
+                turned[pl.ds(j * channels, channels), :] = tap.T
+
+            def step_at(place, k=k, by=by):
+                wide = jnp.concatenate(
+                    [
+                        hidden[k][pl.ds(pl.multiple_of(place + j * by, 16), tile), :]
+                        for j in range(3)
+                    ],
+                    1,
+                )
+                total = jnp.dot(wide, turned[...], preferred_element_type=jnp.float32)
+                value, bent = both_gelu(total)
+                value = value.astype(jnp.bfloat16)
+                active[k][pl.ds(place, tile), :] = value
+                bend[k][pl.ds(place, tile), :] = bent.astype(jnp.bfloat16)
+                update = jnp.dot(
+                    value,
+                    held[k, pl.ds(3 * inner, inner), :],
+                    preferred_element_type=jnp.float32,
+                )
+                return (state[pl.ds(place, tile), :].astype(jnp.float32) + update).astype(
+                    jnp.bfloat16
+                )
+
+            if k < sections - 1:
+
+                def step(i, carry, k=k):
+                    place = pl.multiple_of(i * tile, 16)
+                    new = step_at(place)
+                    state[pl.ds(place, tile), :] = new
+                    value, bent = both_gelu(new.astype(jnp.float32))
+                    ahead = pl.multiple_of(shifts[k + 1] + place, 16)
+                    hidden[k + 1][pl.ds(ahead, tile), :] = value.astype(jnp.bfloat16)
+                    slope[k][pl.ds(place, tile), :] = bent.astype(jnp.bfloat16)
+                    return carry
+
+                lax.fori_loop(0, length // tile, step, 0)
+                keep(hidden[k + 1].at[pl.ds(shifts[k + 1], length)], hidden_out[k + 1])
+                keep(slope[k], slope_out[k])
+            else:
+
+                def away(i, carry):
+                    place = pl.multiple_of((1 - c) * half + i * tile, 16)
+                    state[pl.ds(place, tile), :] = step_at(place)
+                    return carry
+
+                lax.fori_loop(0, steps, away, 0)
+                theirs = state.at[pl.ds(pl.multiple_of((1 - c) * half, 16), half)]
+                last = remote(theirs, top_ref.at[c], tsend, trecv, partner)
+                last.start()
+
+                def here(i, carry):
+                    at = pl.multiple_of(i * tile, 16)
+                    place = pl.multiple_of(c * half + at, 16)
+                    top_ref[c, pl.ds(at, tile), :] = step_at(place)
+                    return carry
+
+                lax.fori_loop(0, steps, here, 0)
+            keep(active[k], active_out[k])
+            keep(bend[k], bend_out[k])
+        for copy in outs:
             copy.wait()
-        for copy in first:
+        last.wait()
+        across.wait_send()
+        for copy in first + second:
             copy.wait_send()
-        for copy in own:
-            copy.wait()
-
-    sems = pltpu.SemaphoreType.DMA((sections - 1, 2))
+
+    bf16 = jnp.bfloat16
+    long = jax.ShapeDtypeStruct((length, channels), bf16)
+    thin = jax.ShapeDtypeStruct((length, inner), bf16)
+    dma = pltpu.SemaphoreType.DMA
+    copies = 4 * sections
+    out = pl.pallas_call(
+        kernel,
+        out_shape=[
+            jax.ShapeDtypeStruct((seqs, half, channels), bf16),
+            jax.ShapeDtypeStruct((sections, rows, channels), bf16),
+        ]
+        + [long] * (2 * sections - 1)
+        + [thin] * (2 * sections),
+        in_specs=[ANY, pl.BlockSpec(memory_space=pltpu.VMEM), ANY, ANY],
+        out_specs=[pl.BlockSpec(memory_space=pltpu.VMEM)] + [ANY] * (4 * sections),
+        scratch_shapes=[
+            pltpu.VMEM((seqs, half, width), jnp.int32),
+            pltpu.VMEM((sections, rows, channels), bf16),
+            pltpu.VMEM((3 * channels, inner), bf16),
+            pltpu.VMEM((length, channels), bf16),
+        ]
+        + [pltpu.VMEM((length + 2 * by, channels), bf16) for by in shifts]
+        + [pltpu.VMEM((length, channels), bf16)] * (sections - 1)
+        + [pltpu.VMEM((length, inner), bf16)] * (2 * sections)
+        + [dma, dma]
+        + [dma((sections - 1,))] * 4
+        + [dma, dma, dma((3,)), dma((copies,))],
+        compiler_params=pltpu.CompilerParams(
+            collective_id=0, has_side_effects=True, vmem_limit_bytes=54 * 2**20
+        ),
+        name="forward_tower",
+    )(bases, stem, taps, proj)
+    top, weights = out[:2]
+    hidden, slope = out[2 : 2 + sections], out[2 + sections : 1 + 2 * sections]
+    active = out[1 + 2 * sections : 1 + 3 * sections]
+    bend = out[1 + 3 * sections :]
+    return top, weights, hidden, slope, active, bend
+
+
+def head(top, targets, head_weight, factor):
+    seqs, half, channels = top.shape
+    tracks = head_weight.shape[1]
+    tile = tile_of(half)
+    steps = half // tile
+
+    def kernel(
+        top_ref, targets_ref, weight_ref, grad_ref, cot_ref, counts, stage, load, send, recv
+    ):
+        s, c = lax.axis_index("section"), lax.axis_index("seq")
+        partner = {"section": s, "seq": 1 - c}
+        loads = []
+        for n, b in enumerate((1 - c, c)):
+            for i in range(steps):
+                loads.append(
+                    pltpu.make_async_copy(
+                        targets_ref.at[b, pl.ds(i * tile, tile)],
+                        counts.at[n * steps + i],
+                        load.at[n * steps + i],
+                    )
+                )
+                loads[-1].start()
+        greet([partner])
+        grad_ref[...] = jnp.zeros_like(grad_ref)
+
+        def run(b, n, store):
+            def step(i, carry):
+                at = pl.multiple_of(i * tile, 16)
+                pltpu.make_async_copy(
+                    targets_ref.at[b, pl.ds(at, tile)], counts.at[n + i], load.at[n + i]
+                ).wait()
+                value, bent = both_gelu(top_ref[b, pl.ds(at, tile), :].astype(jnp.float32))
+                lifted = value.astype(jnp.bfloat16)
+                logits = jnp.dot(lifted, weight_ref[...], preferred_element_type=jnp.float32)
+                drop = jnp.exp(logits) - counts[n + i].astype(jnp.float32)
+                drop = (drop * factor).astype(jnp.bfloat16)
+                grad_ref[...] += contract_rows(lifted, drop)
+                lift = times_transposed(drop, weight_ref[...])
+                store(at, (lift * bent).astype(jnp.bfloat16))
+                return carry
+
+            lax.fori_loop(0, steps, step, 0)
+
+        def away(at, value):
+            stage[pl.ds(at, tile), :] = value
+
+        def here(at, value):
+            cot_ref[c, pl.ds(at, tile), :] = value
+
+        run(1 - c, 0, away)
+        copy = remote(stage, cot_ref.at[c], send, recv, partner)
+        copy.start()
+        run(c, steps, here)
+        copy.wait()
+
+    vmem = pl.BlockSpec(memory_space=pltpu.VMEM)
+    dma = pltpu.SemaphoreType.DMA
     return pl.pallas_call(
         kernel,
         out_shape=[
-            jax.ShapeDtypeStruct((sections,) + conv.shape, conv.dtype),
-            jax.ShapeDtypeStruct((sections,) + proj.shape, proj.dtype),
+            jax.ShapeDtypeStruct((channels, tracks), jnp.float32),
+            jax.ShapeDtypeStruct(top.shape, jnp.bfloat16),
         ],
-        in_specs=[ANY] * 2,
-        out_specs=[ANY] * 2,
-        scratch_shapes=[sems, sems, pltpu.SemaphoreType.DMA((2,)), sems, sems],
-        compiler_params=pltpu.CompilerParams(collective_id=0, has_side_effects=True),
-    )(conv, proj)
-
-
-def exchange(value, sections, seqs, columns, to_head):
-    group = sections * seqs
-
-    def kernel(src, out, send, recv, local):
-        s, c = lax.axis_index("section"), lax.axis_index("seq")
-        me = s * seqs + c
-
-        def part(ref, batch, section):
-            start = pl.multiple_of(section * columns, 16)
-            return ref.at[batch, :, pl.ds(start, columns), :]
-
-        def ends(ps, pc):
-            if to_head:
-                return src.at[pc], part(out, c, s)
-            return part(src, pc, ps), out.at[s, c]
-
-        places = []
-        for k in range(1, group):
-            p = lax.rem(me + k, group)
-            places.append((p // seqs, lax.rem(p, seqs)))
-        peers = [{"section": ps, "seq": pc} for ps, pc in places]
-        greet(peers)
-        copies = []
-        for k, (ps, pc) in enumerate(places):
-            source, target = ends(ps, pc)
-            copies.append(remote(source, target, send.at[k], recv.at[k], peers[k]))
-            copies[-1].start()
-        source, target = ends(s, c)
-        own = pltpu.make_async_copy(source, target, local)
-        own.start()
-        own.wait()
-        for copy in copies:
-            copy.wait()
-
-    q, channels = value.shape[1], value.shape[3]
-    if to_head:
-        shape = (seqs, q, sections * columns, channels)
-    else:
-        shape = (sections, seqs, q, columns, channels)
-    sems = pltpu.SemaphoreType.DMA((group - 1,))
+        in_specs=[vmem, ANY, vmem],
+        out_specs=[vmem, vmem],
+        scratch_shapes=[
+            pltpu.VMEM((seqs * steps, tile, tracks), jnp.int32),
+            pltpu.VMEM((half, channels), jnp.bfloat16),
+            dma((seqs * steps,)),
+            dma,
+            dma,
+        ],
+        compiler_params=pltpu.CompilerParams(
+            collective_id=1, has_side_effects=True, vmem_limit_bytes=48 * 2**20
+        ),
+        name="head",
+    )(top, targets, head_weight)
+
+
+def backward_tower(cot, weights, hidden, slope, active, bend, sections, unit):
+    length, channels = hidden[0].shape
+    inner = active[0].shape[1]
+    tile = tile_of(length)
+    most = unit * 2 ** (sections - 1)
+
+    def kernel(*refs):
+        cot_in, weights_ref = refs[:2]
+        refs = refs[2:]
+        hidden_in, slope_in = refs[:sections], refs[sections : 2 * sections - 1]
+        refs = refs[2 * sections - 1 :]
+        active_in, bend_in = refs[:sections], refs[sections : 2 * sections]
+        out = refs[2 * sections]
+        refs = refs[2 * sections + 1 :]
+        hidden, slope = refs[:sections], refs[sections : 2 * sections - 1]
+        refs = refs[2 * sections - 1 :]
+        active, bend = refs[:sections], refs[sections : 2 * sections]
+        held, grad, pull, sems = refs[2 * sections :]
+        count = [0]
+
+        def fetch(src, dst):
+            copy = pltpu.make_async_copy(src, dst, sems.at[count[0]])
+            count[0] += 1
+            copy.start()
+            return copy
+
+        bring = {}
+        for k in reversed(range(sections)):
+            early = [fetch(weights_ref.at[k], held.at[k])]
+            if k == sections - 1:
+                early.append(fetch(cot_in, grad))
+            early.append(fetch(bend_in[k], bend[k]))
+            early.append(fetch(active_in[k], active[k]))
+            late = [fetch(hidden_in[k], hidden[k])]
+            if k:
+                late.append(fetch(slope_in[k - 1], slope[k - 1]))
+            bring[k] = (early, late)
+        pull[pl.ds(0, most), :] = jnp.zeros((most, inner), jnp.bfloat16)
+        pull[pl.ds(most + length, most), :] = jnp.zeros((most, inner), jnp.bfloat16)
+        out[...] = jnp.zeros_like(out)
+
+        for k in reversed(range(sections)):
+            by = unit * 2**k
+            for copy in bring[k][0]:
+                copy.wait()
+
+            def inward(i, carry, k=k):
+                place = pl.multiple_of(i * tile, 16)
+                here = grad[pl.ds(place, tile), :]
+                back = times_transposed(here, held[k, pl.ds(3 * inner, inner), :])
+                back = back * bend[k][pl.ds(place, tile), :].astype(jnp.float32)
+                pull[pl.ds(pl.multiple_of(most + place, 16), tile), :] = back.astype(jnp.bfloat16)
+                out[k, pl.ds(3 * inner, inner), :] += contract_rows(
+                    active[k][pl.ds(place, tile), :], here
+                )
+                return carry
+
+            lax.fori_loop(0, length // tile, inward, 0)
+            for copy in bring[k][1]:
+                copy.wait()
+
+            def outward(i, carry, k=k, by=by):
+                place = pl.multiple_of(i * tile, 16)
+                there = hidden[k][pl.ds(place, tile), :]
+                total = None
+                for j in range(3):
+                    piece = pull[pl.ds(pl.multiple_of(most + place + (1 - j) * by, 16), tile), :]
+                    rows = pl.ds(j * inner, inner)
+                    out[k, rows, :] += contract_rows(piece, there)
+                    if k:
+                        term = jnp.dot(
+                            piece, held[k, rows, :], preferred_element_type=jnp.float32
+                        )
+                        total = term if total is None else total + term
+                if k:
+                    total = total * slope[k - 1][pl.ds(place, tile), :].astype(jnp.float32)
+                    total = total + grad[pl.ds(place, tile), :].astype(jnp.float32)
+                    grad[pl.ds(place, tile), :] = total.astype(jnp.bfloat16)
+                return carry
+
+            lax.fori_loop(0, length // tile, outward, 0)
+
+    bf16 = jnp.bfloat16
     return pl.pallas_call(
         kernel,
-        out_shape=jax.ShapeDtypeStruct(shape, value.dtype),
-        in_specs=[pl.BlockSpec(memory_space=pltpu.VMEM)],
+        out_shape=jax.ShapeDtypeStruct(
+            (sections, weights.shape[1], channels), jnp.float32
+        ),
+        in_specs=[ANY] * (2 + 4 * sections - 1),
         out_specs=pl.BlockSpec(memory_space=pltpu.VMEM),
-        scratch_shapes=[sems, sems, pltpu.SemaphoreType.DMA],
-        compiler_params=pltpu.CompilerParams(
-            collective_id=1 if to_head else 2, has_side_effects=True, vmem_limit_bytes=16 * 2**20
-        ),
-    )(value)
+        scratch_shapes=[pltpu.VMEM((length, channels), bf16)] * (2 * sections - 1)
+        + [pltpu.VMEM((length, inner), bf16)] * (2 * sections)
+        + [
+            pltpu.VMEM(weights.shape, bf16),
+            pltpu.VMEM((length, channels), bf16),
+            pltpu.VMEM((length + 2 * most, inner), bf16),
+            pltpu.SemaphoreType.DMA((5 * sections,)),
+        ],
+        compiler_params=pltpu.CompilerParams(vmem_limit_bytes=56 * 2**20),
+        name="backward_tower",
+    )(cot, weights, *hidden, *slope, *active, *bend)
 
 
 def sum_gradients(value, sections, zones):
@@ -250,7 +561,7 @@
     return out.reshape(rows, width)
 
 
-def body(bases, targets, stem_weight, conv_weight, proj_weight, head_weight):
+def plain_body(bases, targets, stem_weight, conv_weight, proj_weight, head_weight):
     sections = lax.axis_size("section")
     seqs = lax.axis_size("seq")
     section_number = lax.axis_index("section")
@@ -263,19 +574,8 @@
     blocks = length // unit
     columns = batches * unit // (seqs * sections)
 
-    paired = seqs == 2 and batches == seqs and columns % 16 == 0
-
-    if paired:
-        conv_all, proj_all = gather_weights(
-            conv_weight.reshape(2, -1, conv_weight.shape[-1]),
-            proj_weight.reshape(2, -1, channels),
-            sections,
-        )
-        conv_all = conv_all.reshape((sections,) + conv_weight.shape[1:])
-        proj_all = proj_all.reshape((sections,) + proj_weight.shape[1:])
-    else:
-        conv_all = lax.all_gather(conv_weight, "section", axis=0, tiled=True)
-        proj_all = lax.all_gather(proj_weight, "section", axis=0, tiled=True)
+    conv_all = lax.all_gather(conv_weight, "section", axis=0, tiled=True)
+    proj_all = lax.all_gather(proj_weight, "section", axis=0, tiled=True)
 
     def to_chains(value):
         value = lax.all_to_all(value, "seq", split_axis=1, concat_axis=0, tiled=True)
@@ -302,15 +602,11 @@
         state = (state.astype(jnp.float32) + update).astype(jnp.bfloat16)
 
     lifted = gelu_value(state.astype(jnp.float32)).astype(jnp.bfloat16)
-    if paired:
-        lifted = lifted.reshape(seqs, local_q, columns, channels)
-        lifted = exchange(lifted, sections, seqs, columns, True)
-    else:
-        lifted = lifted.reshape(seqs, local_q, 1, columns, channels)
-        lifted = lax.all_to_all(lifted, "seq", split_axis=0, concat_axis=2, tiled=True)
-        lifted = lifted.reshape(local_q, seqs, 1, columns, channels)
-        lifted = lax.all_gather(lifted, "section", axis=2, tiled=True)
-        lifted = lifted.reshape(local_q, batches, unit, channels).transpose(1, 0, 2, 3)
+    lifted = lifted.reshape(seqs, local_q, 1, columns, channels)
+    lifted = lax.all_to_all(lifted, "seq", split_axis=0, concat_axis=2, tiled=True)
+    lifted = lifted.reshape(local_q, seqs, 1, columns, channels)
+    lifted = lax.all_gather(lifted, "section", axis=2, tiled=True)
+    lifted = lifted.reshape(local_q, batches, unit, channels).transpose(1, 0, 2, 3)
     lifted = lifted.reshape(batches * row_count, channels)
 
     logits = jnp.dot(lifted, head_weight, preferred_element_type=jnp.float32)
@@ -319,15 +615,11 @@
     head_sum = lax.psum(contract_rows(lifted, slope), ("seq", "dp"))
     lift_part = times_transposed(slope, head_weight)
 
-    if paired:
-        lift_part = lift_part.astype(jnp.bfloat16).reshape(batches, local_q, unit, channels)
-        terms = exchange(lift_part, sections, seqs, columns, False)
-        lift_grad = terms.astype(jnp.float32).sum(0).reshape(blocks * columns, channels)
-    else:
-        lift_part = lift_part.reshape(batches, local_q, unit, channels).transpose(1, 0, 2, 3)
-        lift_part = lift_part.reshape(local_q, seqs, sections, columns, channels)
-        lift_part = lax.psum_scatter(lift_part, "section", scatter_dimension=2, tiled=True)
-        lift_grad = to_chains(lift_part.reshape(local_q, seqs, columns, channels))
+    lift_part = lift_part.reshape(batches, local_q, unit, channels).transpose(1, 0, 2, 3)
+    lift_part = lift_part.reshape(local_q, seqs, sections, columns, channels)
+    lift_part = lax.psum_scatter(lift_part, "section", scatter_dimension=2, tiled=True)
+    lift_grad = to_chains(lift_part.reshape(local_q, seqs, columns, channels))
+
 
     grad = (lift_grad * gelu_slope(state.astype(jnp.float32))).astype(jnp.bfloat16)
     parts = []
@@ -348,15 +640,46 @@
             grad.astype(jnp.float32) + hidden_grad * gelu_slope(start_state.astype(jnp.float32))
         ).astype(jnp.bfloat16)
     parts = jnp.stack(parts[::-1])
-    zones = lax.axis_size("dp")
-    if paired and zones > 1 and parts.shape[1] % (16 * zones) == 0:
-        total = sum_gradients(parts, sections, zones)
-    else:
-        total = lax.psum_scatter(parts, "section", scatter_dimension=0, tiled=True)
-        total = lax.psum(total[0], ("seq", "dp"))
+    total = lax.psum_scatter(parts, "section", scatter_dimension=0, tiled=True)
+    total = lax.psum(total[0], ("seq", "dp"))
     taps_width = total.shape[1] - channels
     conv_sum = total[:, :taps_width].T.reshape(conv_weight.shape)
     return conv_sum, total[:, taps_width:][None], head_sum
+
+
+def paired_body(bases, targets, stem_weight, conv_weight, proj_weight, head_weight):
+    sections = lax.axis_size("section")
+    zones = lax.axis_size("dp")
+    batches, half, bin_width = bases.shape
+    channels = stem_weight.shape[1]
+    inner = proj_weight.shape[1]
+    length = batches * half
+    unit = length // 2**sections
+    factor = 1.0 / math.sqrt(batches * zones * length)
+    stem = stem_weight.reshape(bin_width, 4, channels).transpose(1, 0, 2).reshape(-1, channels)
+    taps = conv_weight[0].transpose(0, 2, 1).reshape(3 * inner, channels)
+    top, weights, hidden, slope, active, bend = forward_tower(
+        bases, stem, taps, proj_weight[0], sections, unit
+    )
+    head_part, cot = head(top, targets, head_weight, factor)
+    head_sum = lax.psum(head_part, ("seq", "dp"))
+    cot = cot.reshape(length, channels)
+    parts = backward_tower(cot, weights, hidden, slope, active, bend, sections, unit)
+    total = sum_gradients(parts, sections, zones)
+    conv_sum = total[: 3 * inner].reshape(3, inner, channels).transpose(0, 2, 1)
+    return conv_sum[None], total[3 * inner :][None], head_sum
+
+
+def body(bases, targets, stem_weight, conv_weight, proj_weight, head_weight):
+    sections, zones = lax.axis_size("section"), lax.axis_size("dp")
+    batches, half = bases.shape[:2]
+    inner = proj_weight.shape[1]
+    unit = batches * half // 2**sections
+    paired = lax.axis_size("seq") == 2 and batches == 2 and zones > 1 and sections > 1
+    paired = paired and unit % 16 == 0 and half % 16 == 0 and inner % 16 == 0
+    paired = paired and (4 * inner) % (16 * zones) == 0
+    run = paired_body if paired else plain_body
+    return run(bases, targets, stem_weight, conv_weight, proj_weight, head_weight)
 
 
 def solution(mesh):

time: 225 us -> 177 us (0.79)
  matrix products: 48.5 us -> 0 us
  Pallas kernels: 130 us -> 151 us
  local copies, waits for them, and re-layouts: 22.5 us -> 10.2 us
  other arithmetic: 4.32 us -> 0 us
  starting transfers between devices: 3.47 us -> 0.04 us
    dot_general x26 -> x0, matrix products: 48.5 us -> none  [the longest x9 15.5 us: contract_rows(): lax.dot_general(left_side, right_side, (((0,), (0,)), ((), ())), preferre...]
    pallas_call x3, Pallas kernels: 83.1 us -> 103 us  [the longest x1 52.4 us: forward_tower(): pl.pallas_call(kernel, out_shape=[jax.ShapeDtypeStruct((seqs, half, chann...]
    unnamed x117 -> x7, local copies, waits for them, and re-layouts: 13 us -> 6.57 us
    all_to_all x1 -> x0, starting transfers between devices: 3.43 us -> none  [to_chains(): lax.all_to_all(value, 'seq', split_axis=1, concat_axis=0, tiled=True)]
    slice x9 -> x1, local copies, waits for them, and re-layouts: 3.92 us -> 0.97 us  [paired_body(): conv_sum = total[:3 * inner].reshape(3, inner, channels).transpose(0, 2, 1)]
    convert_element_type x2 -> x0, other arithmetic: 2.62 us -> none  [the longest x1 1.82 us: body(): picked = to_chains(own.astype(jnp.bfloat16))]
    squeeze x3 -> x0, local copies, waits for them, and re-layouts: 2.27 us -> none  [body(): kernel = conv_all[layer]]
  transfers between devices with their start and end apart: 2 -> 1, of which waited for: 1 -> 0; matrix products, arithmetic and copies ran while one was open for 18% -> 1% of each run, Pallas kernels for 34% -> 48%
where the time goes in v1:
time: 177 us; the launch traced here: 175 us
  Pallas kernels  151 us (85%)
  between operations  14.1 us (8%)
  local copies, waits for them, and re-layouts  10.2 us (6%)
    pallas_call x1, Pallas kernels, forward_tower(): pl.pallas_call(kernel, out_shape=[jax.ShapeDtypeStruct((seqs, half, chann...  52.4 us
    pallas_call x1, Pallas kernels, sum_gradients(): pl.pallas_call(kernel, out_shape=jax.ShapeDtypeStruct((2, half, width), j...  47.8 us
    pallas_call x1, Pallas kernels, backward_tower(): pl.pallas_call(kernel, out_shape=jax.ShapeDtypeStruct((sections, weights....  35.4 us
    pallas_call x1, Pallas kernels, head(): pl.pallas_call(kernel, out_shape=[jax.ShapeDtypeStruct((channels, tracks)...  14.9 us
    unnamed x7, local copies, waits for them, and re-layouts  6.57 us
  transfers between devices with their start and end apart: 1, of which 0 were waited for; matrix products, arithmetic and copies ran while one was open for 1% of the time, Pallas kernels for 48%

profile of v1, /device:TPU:0, one launch (start us, length us, event | category | flops | bytes accessed | tf_op | source)
XLA Modules:
  0.0 174.9 jit_solution(12933367510409658004)
XLA Ops:
  7.2 0.0 all-reduce.2.cloned.1.call-start
  7.2 1.1 reshape.24
  8.3 0.0 copy-start.2
  8.3 0.8 copy.9
  9.1 52.4 %forward_tower.1 = (bf16[2,1536,384]{2,1,0:T(8,128)(2,1)}, bf16[4,768,384]{2,1,0:T(8,128)(2,1)}, bf16[3072,384]{1,0:T(8,128)(2,1)}, bf16[3072,384]{1,0:T(8,128)(...) custom-call(s32[2,1536,128]{2,1,0:T(8,128)} %refs_0_.1, ...), custom_call_target="tpu_custom_call" | custom-call | tf_op jit(solution)/shard_map/forward_tower/pallas_call | solution.py:258
  61.5 0.0 copy-done.2
  61.5 14.9 %head.1 = (f32[384,1024]{1,0:T(8,128)}, bf16[2,1536,384]{2,1,0:T(8,128)(2,1)S(1)}) custom-call(bf16[2,1536,384]{2,1,0:T(8,128)(2,1)} %get-tuple-element.22.top_ref, s32[2,1536,1024]{2,1,0:T(8,128)} %targets_ref.1, bf16[384,1024]{1,0:T(8,128)(2,1)S(1)} %copy-done.2), custom_call_target="tpu_custom_call" | custom-call | tf_op jit(solution)/shard_map/head/pallas_call | solution.py:349
  76.4 0.0 copy-start.1
  76.4 1.5 copy-done.1
  77.9 0.0 all-reduce.2.cloned.1.call-update
  77.9 35.4 %backward_tower.1.src = f32[4,768,384]{2,1,0:T(8,128)} custom-call(bf16[3072,384]{1,0:T(8,128)(2,1)} %bitcast.20, bf16[4,768,384]{2,1,0:T(8,128)(2,1)} %get-tuple-element.24.refs_1_, bf16[3072,384]{1,0:T(8,128)(2,1)} %get-tuple-element.25.refs_2_, bf16[3072,384]{1,0:T(8,128)(2,1)} %get-tuple-element.26.refs_3_, bf16[3072,384]{1,0:T(8,128)(2,1)} %get-tuple-element.27.refs_4_, ...), custom_call_target="tpu_custom_call" | custom-call | tf_op jit(solution)/shard_map/backward_tower/pallas_call | solution.py:454
  113.3 0.0 copy-start
  113.4 2.4 %copy-done = f32[4,768,384]{2,1,0:T(8,128)S(1)} copy-done((f32[4,768,384]{2,1,0:T(8,128)S(1)}, f32[4,768,384]{2,1,0:T(8,128)}, u32[]{:S(2)}) %copy-start) | copy-done | bytes 4718616
  115.7 47.8 %shard_map.85 = f32[2,384,384]{2,1,0:T(8,128)S(1)} custom-call(f32[4,768,384]{2,1,0:T(8,128)S(1)} %copy-done), custom_call_target="tpu_custom_call" | custom-call | tf_op jit(solution)/shard_map/pallas_call | solution.py:544
  163.6 1.0 slice.8
  164.5 0.7 slice_bitcast_fusion
  165.3 0.0 all-reduce.2.cloned.1.call-done
  165.3 2.7 %copy.12 = f32[384,1024]{1,0:T(8,128)} copy(f32[384,1024]{1,0:T(8,128)} %all-reduce.2.cloned.1.call-done) | data formatting | bytes 3145728
Async XLA Ops:
  7.2 158.1 %all-reduce.2.cloned.1.call-start = ((), (), s32[]{:S(2)}) async-start(), calls=%async_computation | async-start | bytes 3145728 | tf_op jit(solution)/shard_map/psum | solution.py:665
  8.3 53.2 %copy-start.2 = (bf16[384,1024]{1,0:T(8,128)(2,1)S(1)}, bf16[384,1024]{1,0:T(8,128)(2,1)}, u32[]{:S(2)}) copy-start(bf16[384,1024]{1,0:T(8,128)(2,1)} %weight_ref.1) | copy-start | bytes 2359300
  76.4 1.5 copy-start.1
  113.3 2.4 %copy-start = (f32[4,768,384]{2,1,0:T(8,128)S(1)}, f32[4,768,384]{2,1,0:T(8,128)}, u32[]{:S(2)}) copy-start(f32[4,768,384]{2,1,0:T(8,128)} %backward_tower.1.src) | copy-start | bytes 14155780
Sparse Core Ops, SparseCore 0:
  78.0 67.9 all-reduce.1

commit v2 on v1

--- a/solution.py
+++ b/solution.py
@@ -368,197 +368,322 @@
     )(top, targets, head_weight)
 
 
-def backward_tower(cot, weights, hidden, slope, active, bend, sections, unit):
+def backward_tower(head_part, cot, weights, hidden, slope, active, bend, sections, zones, unit):
     length, channels = hidden[0].shape
     inner = active[0].shape[1]
-    tile = tile_of(length)
+    rows = weights.shape[1]
+    part = rows // 2
+    quarter = part // sections
+    strip = quarter // zones
+    tracks = head_part.shape[1]
+    side = head_part.shape[0] // 2
+    band = side // zones
+    tile = length // 2
     most = unit * 2 ** (sections - 1)
+    f32, bf16 = jnp.float32, jnp.bfloat16
 
     def kernel(*refs):
-        cot_in, weights_ref = refs[:2]
-        refs = refs[2:]
+        head_ref, cot_ref, weights_ref = refs[:3]
+        refs = refs[3:]
         hidden_in, slope_in = refs[:sections], refs[sections : 2 * sections - 1]
         refs = refs[2 * sections - 1 :]
         active_in, bend_in = refs[:sections], refs[sections : 2 * sections]
-        out = refs[2 * sections]
-        refs = refs[2 * sections + 1 :]
-        hidden, slope = refs[:sections], refs[sections : 2 * sections - 1]
-        refs = refs[2 * sections - 1 :]
-        active, bend = refs[:sections], refs[sections : 2 * sections]
-        held, grad, pull, sems = refs[2 * sections :]
+        refs = refs[2 * sections :]
+        out, head_out = refs[:2]
+        hidden, slope, active, bend = refs[2:4], refs[4:6], refs[6:8], refs[8:10]
+        held, grad, pull, sums, load = refs[10:15]
+        met, wire, came, total, zcame, final = refs[15:21]
+        hmet, hsum, hcame = refs[21:24]
+        sems = refs[24:]
+
+        s, c, d = (lax.axis_index(name) for name in ("section", "seq", "dp"))
+        partner = {"section": s, "seq": 1 - c, "dp": d}
+        order = [lax.rem(s + k, sections) for k in range(1, sections)]
+        across = [{"section": o, "seq": c, "dp": d} for o in order]
+        levels = [lax.rem(d + k, zones) for k in range(1, zones)]
+        along = [{"section": s, "seq": c, "dp": z} for z in levels]
         count = [0]
 
         def fetch(src, dst):
-            copy = pltpu.make_async_copy(src, dst, sems.at[count[0]])
+            copy = pltpu.make_async_copy(src, dst, load.at[count[0]])
             count[0] += 1
             copy.start()
             return copy
 
         bring = {}
-        for k in reversed(range(sections)):
-            early = [fetch(weights_ref.at[k], held.at[k])]
-            if k == sections - 1:
-                early.append(fetch(cot_in, grad))
-            early.append(fetch(bend_in[k], bend[k]))
-            early.append(fetch(active_in[k], active[k]))
-            late = [fetch(hidden_in[k], hidden[k])]
+
+        def prefetch(k):
+            slot = k % 2
+            early = [
+                fetch(weights_ref.at[k], held.at[k]),
+                fetch(bend_in[k], bend[slot]),
+                fetch(active_in[k], active[slot]),
+            ]
+            late = [fetch(hidden_in[k], hidden[slot])]
             if k:
-                late.append(fetch(slope_in[k - 1], slope[k - 1]))
+                late.append(fetch(slope_in[k - 1], slope[slot]))
             bring[k] = (early, late)
-        pull[pl.ds(0, most), :] = jnp.zeros((most, inner), jnp.bfloat16)
-        pull[pl.ds(most + length, most), :] = jnp.zeros((most, inner), jnp.bfloat16)
-        out[...] = jnp.zeros_like(out)
-
+
+        prefetch(sections - 1)
+        greet([partner] + across + along)
+
+        sends = []
+
+        def launch(src, dst, pair, index, peer):
+            copy = remote(src, dst, sems[2 * pair].at[index], sems[2 * pair + 1].at[index], peer)
+            copy.start()
+            sends.append(copy)
+            return copy
+
+        def block(base, size, number):
+            return pl.ds(pl.multiple_of(base + number * size, 8), size)
+
+        flight = {}
+
+        def swap(k):
+            far = sums.at[k, block(0, part, 1 - c)]
+            flight[k] = [launch(far, met.at[k], 0, k, partner)]
+
+        def spread(k):
+            flight[k][0].wait_recv()
+            flight[k] = []
+
+            def both(o):
+                return met[k, block(0, quarter, o), :] + sums[k, block(c * part, quarter, o), :]
+
+            for n, o in enumerate(order):
+                wire[k, n] = both(o).astype(bf16)
+                flight[k].append(
+                    launch(wire.at[k, n], came.at[k, n], 1, k * (sections - 1) + n, across[n])
+                )
+            total[k] = both(s)
+
+        def climb(k):
+            for n, copy in enumerate(flight[k]):
+                copy.wait_recv()
+            value = total[k]
+            for n in range(sections - 1):
+                value = value + came[k, n].astype(f32)
+            total[k] = value
+            flight[k] = []
+            for n, z in enumerate(levels):
+                piece = total.at[k, block(0, strip, z)]
+                flight[k].append(
+                    launch(piece, zcame.at[k, n], 2, k * (zones - 1) + n, along[n])
+                )
+
+        def level(k):
+            for copy in flight[k]:
+                copy.wait_recv()
+            value = total[k, block(0, strip, d), :]
+            for n in range(zones - 1):
+                value = value + zcame[k, n]
+            final[k, block(0, strip, d), :] = value
+            mine = final.at[k, block(0, strip, d)]
+            flight[k] = [
+                launch(mine, mine, 3, k * (zones - 1) + n, peer) for n, peer in enumerate(along)
+            ]
+
+        def home(k):
+            owner = {"section": k, "seq": c, "dp": d}
+            index = lax.rem(s + 2 * sections - k - 1, sections)
+            place = out.at[block(c * part, quarter, s)]
+            return remote(final.at[k], place, sems[8].at[k], sems[9].at[index], owner)
+
+        def deliver(k):
+            for copy in flight[k]:
+                copy.wait_recv()
+
+            @pl.when(s != k)
+            def _():
+                home(k).start()
+
+            @pl.when(s == k)
+            def _():
+                out[block(c * part, quarter, s), :] = final[k]
+                relay(0, s).start()
+
+        def relay(n, source):
+            piece = out.at[block(c * part, quarter, source)]
+            return remote(piece, piece, sems[10].at[n], sems[11].at[n], partner)
+
+        def hand(k):
+            @pl.when(s == k)
+            def _():
+                for n, o in enumerate(order):
+                    piece = out.at[block(c * part, quarter, o)]
+                    remote(final.at[k], piece, sems[8].at[k], sems[9].at[n], across[n]).wait_recv()
+                    relay(n + 1, o).start()
+
+        def settle(k):
+            @pl.when(s != k)
+            def _():
+                home(k).wait_send()
+
+            @pl.when(s == k)
+            def _():
+                for n, o in enumerate([s] + order):
+                    relay(n, o).wait()
+
+        def head_swap():
+            far = head_ref.at[block(0, side, 1 - c)]
+            flight["h"] = [launch(far, hmet, 6, 0, partner)]
+
+        def head_climb():
+            flight["h"][0].wait_recv()
+            hsum[...] = hmet[...] + head_ref[block(0, side, c), :]
+            flight["h"] = [
+                launch(hsum.at[block(0, band, z)], hcame.at[n], 7, n, along[n])
+                for n, z in enumerate(levels)
+            ]
+
+        def head_level():
+            for copy in flight["h"]:
+                copy.wait_recv()
+            value = hsum[block(0, band, d), :]
+            for n in range(zones - 1):
+                value = value + hcame[n]
+            head_out[block(c * side, band, d), :] = value
+            mine = head_out.at[block(c * side, band, d)]
+            flight["h"] = [launch(mine, mine, 8, n, peer) for n, peer in enumerate(along)]
+            flight["r"] = [launch(mine, mine, 9, 0, partner)]
+
+        def head_hand():
+            for n, copy in enumerate(flight["h"]):
+                copy.wait_recv()
+                source = lax.rem(d + zones - 1 - n, zones)
+                piece = head_out.at[block(c * side, band, source)]
+                flight["r"].append(launch(piece, piece, 9, n + 1, partner))
+
+        head_swap()
+        pull[pl.ds(0, most), :] = jnp.zeros((most, inner), bf16)
+        pull[pl.ds(most + length, most), :] = jnp.zeros((most, inner), bf16)
+        sums[...] = jnp.zeros_like(sums)
+
+        top = sections - 1
         for k in reversed(range(sections)):
             by = unit * 2**k
+            slot = k % 2
+            above = cot_ref if k == top else grad
+            if k:
+                prefetch(k - 1)
             for copy in bring[k][0]:
                 copy.wait()
 
-            def inward(i, carry, k=k):
+            def inward(i, carry, k=k, slot=slot, above=above):
                 place = pl.multiple_of(i * tile, 16)
-                here = grad[pl.ds(place, tile), :]
+                here = above[pl.ds(place, tile), :]
                 back = times_transposed(here, held[k, pl.ds(3 * inner, inner), :])
-                back = back * bend[k][pl.ds(place, tile), :].astype(jnp.float32)
-                pull[pl.ds(pl.multiple_of(most + place, 16), tile), :] = back.astype(jnp.bfloat16)
-                out[k, pl.ds(3 * inner, inner), :] += contract_rows(
-                    active[k][pl.ds(place, tile), :], here
+                back = back * bend[slot][pl.ds(place, tile), :].astype(f32)
+                pull[pl.ds(pl.multiple_of(most + place, 16), tile), :] = back.astype(bf16)
+                sums[k, pl.ds(3 * inner, inner), :] += contract_rows(
+                    active[slot][pl.ds(place, tile), :], here
                 )
                 return carry
 
             lax.fori_loop(0, length // tile, inward, 0)
+            if k == top:
+                head_climb()
+            else:
+                if k + 3 <= top:
+                    hand(k + 3)
+                if k + 2 <= top:
+                    level(k + 2)
+                spread(k + 1)
+                if k == top - 2:
+                    head_level()
             for copy in bring[k][1]:
                 copy.wait()
 
-            def outward(i, carry, k=k, by=by):
+            def outward(i, carry, k=k, by=by, slot=slot, above=above):
                 place = pl.multiple_of(i * tile, 16)
-                there = hidden[k][pl.ds(place, tile), :]
-                total = None
+                there = hidden[slot][pl.ds(place, tile), :]
+                value = None
                 for j in range(3):
                     piece = pull[pl.ds(pl.multiple_of(most + place + (1 - j) * by, 16), tile), :]
-                    rows = pl.ds(j * inner, inner)
-                    out[k, rows, :] += contract_rows(piece, there)
+                    span = pl.ds(j * inner, inner)
+                    sums[k, span, :] += contract_rows(piece, there)
                     if k:
-                        term = jnp.dot(
-                            piece, held[k, rows, :], preferred_element_type=jnp.float32
-                        )
-                        total = term if total is None else total + term
+                        term = jnp.dot(piece, held[k, span, :], preferred_element_type=f32)
+                        value = term if value is None else value + term
                 if k:
-                    total = total * slope[k - 1][pl.ds(place, tile), :].astype(jnp.float32)
-                    total = total + grad[pl.ds(place, tile), :].astype(jnp.float32)
-                    grad[pl.ds(place, tile), :] = total.astype(jnp.bfloat16)
+                    value = value * slope[slot][pl.ds(place, tile), :].astype(f32)
+                    value = value + above[pl.ds(place, tile), :].astype(f32)
+                    grad[pl.ds(place, tile), :] = value.astype(bf16)
                 return carry
 
             lax.fori_loop(0, length // tile, outward, 0)
-
-    bf16 = jnp.bfloat16
+            swap(k)
+            if k + 1 <= top:
+                climb(k + 1)
+            if k + 2 <= top:
+                deliver(k + 2)
+
+        spread(0)
+        level(1)
+        hand(2)
+        climb(0)
+        deliver(1)
+        level(0)
+        hand(1)
+        deliver(0)
+        head_hand()
+        hand(0)
+        for copy in flight["r"]:
+            copy.wait_recv()
+        for k in range(sections):
+            settle(k)
+        for copy in sends:
+            copy.wait_send()
+
+    dma = pltpu.SemaphoreType.DMA
+
+    def pair(count):
+        return [dma((count,))] * 2
+
+    long, thin = pltpu.VMEM((length, channels), bf16), pltpu.VMEM((length, inner), bf16)
+    vmem = pl.BlockSpec(memory_space=pltpu.VMEM)
     return pl.pallas_call(
         kernel,
-        out_shape=jax.ShapeDtypeStruct(
-            (sections, weights.shape[1], channels), jnp.float32
-        ),
-        in_specs=[ANY] * (2 + 4 * sections - 1),
-        out_specs=pl.BlockSpec(memory_space=pltpu.VMEM),
-        scratch_shapes=[pltpu.VMEM((length, channels), bf16)] * (2 * sections - 1)
-        + [pltpu.VMEM((length, inner), bf16)] * (2 * sections)
+        out_shape=[
+            jax.ShapeDtypeStruct((rows, channels), f32),
+            jax.ShapeDtypeStruct(head_part.shape, f32),
+        ],
+        in_specs=[vmem, vmem] + [ANY] * (4 * sections),
+        out_specs=[vmem, vmem],
+        scratch_shapes=[long] * 4
+        + [thin] * 4
         + [
             pltpu.VMEM(weights.shape, bf16),
-            pltpu.VMEM((length, channels), bf16),
+            long,
             pltpu.VMEM((length + 2 * most, inner), bf16),
-            pltpu.SemaphoreType.DMA((5 * sections,)),
-        ],
-        compiler_params=pltpu.CompilerParams(vmem_limit_bytes=56 * 2**20),
+            pltpu.VMEM((sections, rows, channels), f32),
+            dma((5 * sections,)),
+            pltpu.VMEM((sections, part, channels), f32),
+            pltpu.VMEM((sections, sections - 1, quarter, channels), bf16),
+            pltpu.VMEM((sections, sections - 1, quarter, channels), bf16),
+            pltpu.VMEM((sections, quarter, channels), f32),
+            pltpu.VMEM((sections, zones - 1, strip, channels), f32),
+            pltpu.VMEM((sections, quarter, channels), f32),
+            pltpu.VMEM((side, tracks), f32),
+            pltpu.VMEM((side, tracks), f32),
+            pltpu.VMEM((zones - 1, band, tracks), f32),
+        ]
+        + pair(sections)
+        + pair(sections * (sections - 1))
+        + pair(sections * (zones - 1))
+        + pair(sections * (zones - 1))
+        + [dma((sections,)), dma((sections,))]
+        + pair(sections)
+        + pair(1)
+        + pair(zones - 1)
+        + pair(zones - 1)
+        + pair(zones),
+        compiler_params=pltpu.CompilerParams(
+            collective_id=2, has_side_effects=True, vmem_limit_bytes=56 * 2**20
+        ),
         name="backward_tower",
-    )(cot, weights, *hidden, *slope, *active, *bend)
-
-
-def sum_gradients(value, sections, zones):
-    rows, width = value.shape[1:]
-    half = rows // 2
-    piece = half // zones
-
-    def kernel(
-        src, out, met, wire, came, total, zcame, s0, r0, s1, r1, s2, r2, s3, r3, s4, r4
-    ):
-        s, c, d = (lax.axis_index(name) for name in ("section", "seq", "dp"))
-        partner = {"section": s, "seq": 1 - c, "dp": d}
-        order = [lax.rem(s + k, sections) for k in range(1, sections + 1)]
-        across = [{"section": o, "seq": c, "dp": d} for o in order[:-1]]
-        levels = [lax.rem(d + k, zones) for k in range(1, zones)]
-        along = [{"section": s, "seq": c, "dp": z} for z in levels]
-        greet([partner] + across + along)
-
-        def strip(z):
-            return pl.ds(pl.multiple_of(z * piece, 8), piece)
-
-        def far(o):
-            return src.at[o, pl.ds(pl.multiple_of((1 - c) * half, 8), half), :]
-
-        def near(o):
-            return src[o, pl.ds(pl.multiple_of(c * half, 8), half), :]
-
-        pair = [remote(far(o), met.at[k], s0.at[k], r0.at[k], partner) for k, o in enumerate(order)]
-        for copy in pair:
-            copy.start()
-        hops = []
-        for k, peer in enumerate(across):
-            pair[k].wait_recv()
-            wire[k] = (met[k] + near(order[k])).astype(wire.dtype)
-            hops.append(remote(wire.at[k], came.at[k], s1.at[k], r1.at[k], peer))
-            hops[-1].start()
-        pair[sections - 1].wait_recv()
-        total[...] = met[sections - 1] + near(order[sections - 1])
-        for k, copy in enumerate(hops):
-            copy.wait_recv()
-            total[...] += came[k].astype(jnp.float32)
-        climbs = []
-        for k, peer in enumerate(along):
-            climbs.append(
-                remote(total.at[strip(levels[k])], zcame.at[k], s2.at[k], r2.at[k], peer)
-            )
-            climbs[-1].start()
-        done = total[strip(d), :]
-        for k, copy in enumerate(climbs):
-            copy.wait_recv()
-            done = done + zcame[k]
-        out[c, strip(d), :] = done
-
-        mine = out.at[c, strip(d)]
-        backs = [remote(mine, mine, s3.at[k], r3.at[k], peer) for k, peer in enumerate(along)]
-        for copy in backs:
-            copy.start()
-        ends = [remote(mine, mine, s4.at[0], r4.at[0], partner)]
-        ends[0].start()
-        for k in range(zones - 1):
-            backs[k].wait_recv()
-            landed = out.at[c, strip(lax.rem(d + zones - 1 - k, zones))]
-            ends.append(remote(landed, landed, s4.at[k + 1], r4.at[k + 1], partner))
-            ends[-1].start()
-        for copy in ends:
-            copy.wait()
-        for copy in pair + hops + climbs + backs:
-            copy.wait_send()
-
-    def dma(count):
-        return [pltpu.SemaphoreType.DMA((count,))] * 2
-
-    out = pl.pallas_call(
-        kernel,
-        out_shape=jax.ShapeDtypeStruct((2, half, width), jnp.float32),
-        in_specs=[pl.BlockSpec(memory_space=pltpu.VMEM)],
-        out_specs=pl.BlockSpec(memory_space=pltpu.VMEM),
-        scratch_shapes=[
-            pltpu.VMEM((sections, half, width), jnp.float32),
-            pltpu.VMEM((sections - 1, half, width), jnp.bfloat16),
-            pltpu.VMEM((sections - 1, half, width), jnp.bfloat16),
-            pltpu.VMEM((half, width), jnp.float32),
-            pltpu.VMEM((zones - 1, piece, width), jnp.float32),
-        ]
-        + dma(sections) + dma(sections - 1) + dma(zones - 1) + dma(zones - 1) + dma(zones),
-        compiler_params=pltpu.CompilerParams(
-            collective_id=3, has_side_effects=True, vmem_limit_bytes=40 * 2**20
-        ),
-    )(value)
-    return out.reshape(rows, width)
+    )(head_part, cot, weights, *hidden, *slope, *active, *bend)
 
 
 def plain_body(bases, targets, stem_weight, conv_weight, proj_weight, head_weight):
@@ -662,10 +787,10 @@
         bases, stem, taps, proj_weight[0], sections, unit
     )
     head_part, cot = head(top, targets, head_weight, factor)
-    head_sum = lax.psum(head_part, ("seq", "dp"))
     cot = cot.reshape(length, channels)
-    parts = backward_tower(cot, weights, hidden, slope, active, bend, sections, unit)
-    total = sum_gradients(parts, sections, zones)
+    total, head_sum = backward_tower(
+        head_part, cot, weights, hidden, slope, active, bend, sections, zones, unit
+    )
     conv_sum = total[: 3 * inner].reshape(3, inner, channels).transpose(0, 2, 1)
     return conv_sum[None], total[3 * inner :][None], head_sum
 
@@ -677,7 +802,9 @@
     unit = batches * half // 2**sections
     paired = lax.axis_size("seq") == 2 and batches == 2 and zones > 1 and sections > 1
     paired = paired and unit % 16 == 0 and half % 16 == 0 and inner % 16 == 0
-    paired = paired and (4 * inner) % (16 * zones) == 0
+    paired = paired and (2 * inner) % (16 * sections) == 0
+    paired = paired and (2 * inner) % (8 * sections * zones) == 0
+    paired = paired and stem_weight.shape[1] % (16 * zones) == 0
     run = paired_body if paired else plain_body
     return run(bases, targets, stem_weight, conv_weight, proj_weight, head_weight)
 

time: 177 us -> 164 us (0.927); the launches traced: 175 us -> 164 us
  between operations: 14.1 us -> 0.69 us
  Pallas kernels: 151 us -> 154 us
    pallas_call x2 -> x1, Pallas kernels: 83.3 us -> 87.6 us  [backward_tower(): pl.pallas_call(kernel, out_shape=[jax.ShapeDtypeStruct((rows, channels),...]
    unnamed x7 -> x9, local copies, waits for them, and re-layouts: 6.57 us -> 3.67 us
  transfers between devices with their start and end apart: 1 -> 0, of which waited for: 0 -> 0; matrix products, arithmetic and copies ran while one was open for 1% -> 0% of each run, Pallas kernels for 48% -> 0%
where the time goes in v2:
time: 164 us
  Pallas kernels  154 us (94%)
  local copies, waits for them, and re-layouts  9.5 us (6%)
    pallas_call x1, Pallas kernels, backward_tower(): pl.pallas_call(kernel, out_shape=[jax.ShapeDtypeStruct((rows, channels),...  87.6 us
    pallas_call x1, Pallas kernels, forward_tower(): pl.pallas_call(kernel, out_shape=[jax.ShapeDtypeStruct((seqs, half, chann...  52.3 us
    pallas_call x1, Pallas kernels, head(): pl.pallas_call(kernel, out_shape=[jax.ShapeDtypeStruct((channels, tracks)...  13.8 us
    unnamed x9, local copies, waits for them, and re-layouts  3.67 us

profile of v2, /device:TPU:0, one launch (start us, length us, event | category | flops | bytes accessed | tf_op | source)
XLA Modules:
  0.0 163.9 jit_solution(3017520584368394212)
XLA Ops:
  0.6 1.1 reshape.21
  1.7 0.0 copy-start.2
  1.7 0.8 copy.9
  2.5 52.3 %forward_tower.1 = (bf16[2,1536,384]{2,1,0:T(8,128)(2,1)}, bf16[4,768,384]{2,1,0:T(8,128)(2,1)}, bf16[3072,384]{1,0:T(8,128)(2,1)}, bf16[3072,384]{1,0:T(8,128)(...) custom-call(s32[2,1536,128]{2,1,0:T(8,128)} %refs_0_.1, ...), custom_call_target="tpu_custom_call" | custom-call | tf_op jit(solution)/shard_map/forward_tower/pallas_call | solution.py:258
  54.9 0.0 copy-done.2
  54.9 13.8 %head.1 = (f32[384,1024]{1,0:T(8,128)S(1)}, bf16[2,1536,384]{2,1,0:T(8,128)(2,1)S(1)}) custom-call(bf16[2,1536,384]{2,1,0:T(8,128)(2,1)} %get-tuple-element.24.top_ref, s32[2,1536,1024]{2,1,0:T(8,128)} %targets_ref.1, bf16[384,1024]{1,0:T(8,128)(2,1)S(1)} %copy-done.2), custom_call_target="tpu_custom_call" | custom-call | tf_op jit(solution)/shard_map/head/pallas_call | solution.py:349
  68.7 0.0 copy-start
  68.7 1.4 copy-done
  70.0 0.0 copy-start.1
  70.0 1.1 copy-done.1
  71.2 87.6 %backward_tower.1 = (f32[768,384]{1,0:T(8,128)}, f32[384,1024]{1,0:T(8,128)}) custom-call(f32[384,1024]{1,0:T(8,128)} %copy-done.1, bf16[3072,384]{1,0:T(8,128)(2,1)} %bitcast.17, bf16[4,768,384]{2,1,0:T(8,128)(2,1)} %get-tuple-element.27.refs_2_, bf16[3072,384]{1,0:T(8,128)(2,1)} %get-tuple-element.28.refs_3_, bf16[3072,384]{1,0:T(8,128)(2,1)} %get-tuple-element.29.refs_4_, ...), custom_call_target="tpu_custom_call" | custom-call | tf_op jit(solution)/shard_map/backward_tower/pallas_call | solution.py:646
  158.8 0.0 copy-start.3
  158.8 1.8 %slice_bitcast_fusion = f32[1,192,384]{2,1,0:T(8,128)} fusion(f32[768,384]{1,0:T(8,128)} %get-tuple-element.43), kind=kLoop, calls=%fused_computation | loop fusion | bytes 589824 | tf_op jit(solution)/shard_map/broadcast_in_dim | solution.py:795
  160.6 2.1 %slice.6 = f32[576,384]{1,0:T(8,128)} slice(f32[768,384]{1,0:T(8,128)} %get-tuple-element.43), slice={[0:576], [0:384]} | slice | bytes 1769472 | tf_op jit(solution)/shard_map/slice | solution.py:794
  162.8 0.0 copy-done.3
  162.8 1.1 copy.11
Async XLA Ops:
  1.7 53.2 %copy-start.2 = (bf16[384,1024]{1,0:T(8,128)(2,1)S(1)}, bf16[384,1024]{1,0:T(8,128)(2,1)}, u32[]{:S(2)}) copy-start(bf16[384,1024]{1,0:T(8,128)(2,1)} %weight_ref.1) | copy-start | bytes 2359300
  68.7 1.4 copy-start
  70.0 1.1 copy-start.1
  158.8 4.0 %copy-start.3 = (f32[384,1024]{1,0:T(8,128)S(1)}, f32[384,1024]{1,0:T(8,128)}, u32[]{:S(2)}) copy-start(f32[384,1024]{1,0:T(8,128)} %get-tuple-element.50) | copy-start | bytes 4718596

commit v3 on v2

--- a/solution.py
+++ b/solution.py
@@ -374,10 +374,9 @@
     rows = weights.shape[1]
     part = rows // 2
     quarter = part // sections
-    strip = quarter // zones
+    levels = zones.bit_length() - 1
     tracks = head_part.shape[1]
     side = head_part.shape[0] // 2
-    band = side // zones
     tile = length // 2
     most = unit * 2 ** (sections - 1)
     f32, bf16 = jnp.float32, jnp.bfloat16
@@ -400,8 +399,10 @@
         partner = {"section": s, "seq": 1 - c, "dp": d}
         order = [lax.rem(s + k, sections) for k in range(1, sections)]
         across = [{"section": o, "seq": c, "dp": d} for o in order]
-        levels = [lax.rem(d + k, zones) for k in range(1, zones)]
-        along = [{"section": s, "seq": c, "dp": z} for z in levels]
+        bits = [lax.rem(d // 2**t, 2) for t in range(levels)]
+        along = [
+            {"section": s, "seq": c, "dp": d + 2**t * (1 - 2 * bits[t])} for t in range(levels)
+        ]
         count = [0]
 
         def fetch(src, dst):
@@ -458,31 +459,46 @@
                 )
             total[k] = both(s)
 
-        def climb(k):
-            for n, copy in enumerate(flight[k]):
-                copy.wait_recv()
-            value = total[k]
-            for n in range(sections - 1):
-                value = value + came[k, n].astype(f32)
-            total[k] = value
-            flight[k] = []
-            for n, z in enumerate(levels):
-                piece = total.at[k, block(0, strip, z)]
-                flight[k].append(
-                    launch(piece, zcame.at[k, n], 2, k * (zones - 1) + n, along[n])
-                )
-
-        def level(k):
+        def kept(span, t):
+            base = 0
+            for step in range(t):
+                base = base + bits[step] * (span >> (step + 1))
+            return base
+
+        def landing(span, t):
+            return pl.ds(span - (span >> t), span >> (t + 1))
+
+        def climb(k, t):
             for copy in flight[k]:
                 copy.wait_recv()
-            value = total[k, block(0, strip, d), :]
-            for n in range(zones - 1):
-                value = value + zcame[k, n]
-            final[k, block(0, strip, d), :] = value
-            mine = final.at[k, block(0, strip, d)]
+            if t == 0:
+                value = total[k]
+                for n in range(sections - 1):
+                    value = value + came[k, n].astype(f32)
+                total[k] = value
+            else:
+                mine = block(kept(quarter, t), quarter >> t, 0)
+                total[k, mine, :] = total[k, mine, :] + zcame[k, landing(quarter, t - 1), :]
+            size = quarter >> (t + 1)
+            away = block(kept(quarter, t), size, 1 - bits[t])
             flight[k] = [
-                launch(mine, mine, 3, k * (zones - 1) + n, peer) for n, peer in enumerate(along)
+                launch(
+                    total.at[k, away],
+                    zcame.at[k, landing(quarter, t)],
+                    2,
+                    k * levels + t,
+                    along[t],
+                )
             ]
+
+        def level(k, t):
+            for copy in flight[k]:
+                copy.wait_recv()
+            mine = block(kept(quarter, t + 1), quarter >> (t + 1), 0)
+            if t == levels - 1:
+                final[k, mine, :] = total[k, mine, :] + zcame[k, landing(quarter, t), :]
+            piece = final.at[k, mine]
+            flight[k] = [launch(piece, piece, 3, k * levels + t, along[t])]
 
         def home(k):
             owner = {"section": k, "seq": c, "dp": d}
@@ -529,31 +545,43 @@
             far = head_ref.at[block(0, side, 1 - c)]
             flight["h"] = [launch(far, hmet, 6, 0, partner)]
 
-        def head_climb():
+        def head_climb(t):
             flight["h"][0].wait_recv()
-            hsum[...] = hmet[...] + head_ref[block(0, side, c), :]
+            if t == 0:
+                hsum[...] = hmet[...] + head_ref[block(0, side, c), :]
+            else:
+                mine = block(kept(side, t), side >> t, 0)
+                hsum[mine, :] = hsum[mine, :] + hcame[landing(side, t - 1), :]
+            away = block(kept(side, t), side >> (t + 1), 1 - bits[t])
             flight["h"] = [
-                launch(hsum.at[block(0, band, z)], hcame.at[n], 7, n, along[n])
-                for n, z in enumerate(levels)
+                launch(hsum.at[away], hcame.at[landing(side, t)], 7, t, along[t])
             ]
 
-        def head_level():
-            for copy in flight["h"]:
-                copy.wait_recv()
-            value = hsum[block(0, band, d), :]
-            for n in range(zones - 1):
-                value = value + hcame[n]
-            head_out[block(c * side, band, d), :] = value
-            mine = head_out.at[block(c * side, band, d)]
-            flight["h"] = [launch(mine, mine, 8, n, peer) for n, peer in enumerate(along)]
-            flight["r"] = [launch(mine, mine, 9, 0, partner)]
+        flight["r"] = []
+
+        def pass_on(start, size):
+            piece = head_out.at[block(c * side + start, size, 0)]
+            flight["r"].append(launch(piece, piece, 9, len(flight["r"]), partner))
+
+        def other(span, t):
+            return kept(span, t) + (1 - bits[t]) * (span >> (t + 1))
+
+        def head_level(t):
+            flight["h"][0].wait_recv()
+            start, size = kept(side, t + 1), side >> (t + 1)
+            place = block(c * side + start, size, 0)
+            if t == levels - 1:
+                mine = block(start, size, 0)
+                head_out[place, :] = hsum[mine, :] + hcame[landing(side, t), :]
+                pass_on(start, size)
+            else:
+                pass_on(other(side, t + 1), side >> (t + 2))
+            piece = head_out.at[place]
+            flight["h"] = [launch(piece, piece, 8, t, along[t])]
 
         def head_hand():
-            for n, copy in enumerate(flight["h"]):
-                copy.wait_recv()
-                source = lax.rem(d + zones - 1 - n, zones)
-                piece = head_out.at[block(c * side, band, source)]
-                flight["r"].append(launch(piece, piece, 9, n + 1, partner))
+            flight["h"][0].wait_recv()
+            pass_on(other(side, 0), side // 2)
 
         head_swap()
         pull[pl.ds(0, most), :] = jnp.zeros((most, inner), bf16)
@@ -561,6 +589,33 @@
         sums[...] = jnp.zeros_like(sums)
 
         top = sections - 1
+        stages = {}
+        for k in range(sections):
+            line = [lambda k=k: swap(k), lambda k=k: spread(k)]
+            line += [lambda k=k, t=t: climb(k, t) for t in range(levels)]
+            line += [lambda k=k, t=t: level(k, t) for t in reversed(range(levels))]
+            stages[k] = line + [lambda k=k: deliver(k), lambda k=k: hand(k)]
+        line = [lambda t=t: head_climb(t) for t in range(levels)]
+        line += [lambda t=t: head_level(t) for t in reversed(range(levels))]
+        stages["h"] = line + [head_hand]
+        marks = {}
+
+        def plan(name, at, gap, until):
+            while at <= until and stages[name]:
+                marks.setdefault(at, []).append(stages[name].pop(0))
+                at += gap
+
+        ends = 4 * sections - 1
+        for k in reversed(range(sections)):
+            plan(k, 4 * (top - k) + 3, 2, ends)
+        plan("h", 1, 4, ends)
+        clock = [0]
+
+        def tick():
+            for stage in marks.get(clock[0], []):
+                stage()
+            clock[0] += 1
+
         for k in reversed(range(sections)):
             by = unit * 2**k
             slot = k % 2
@@ -570,37 +625,28 @@
             for copy in bring[k][0]:
                 copy.wait()
 
-            def inward(i, carry, k=k, slot=slot, above=above):
-                place = pl.multiple_of(i * tile, 16)
+            def inward(i, k=k, slot=slot, above=above):
+                place = i * tile
                 here = above[pl.ds(place, tile), :]
                 back = times_transposed(here, held[k, pl.ds(3 * inner, inner), :])
                 back = back * bend[slot][pl.ds(place, tile), :].astype(f32)
-                pull[pl.ds(pl.multiple_of(most + place, 16), tile), :] = back.astype(bf16)
+                pull[pl.ds(most + place, tile), :] = back.astype(bf16)
                 sums[k, pl.ds(3 * inner, inner), :] += contract_rows(
                     active[slot][pl.ds(place, tile), :], here
                 )
-                return carry
-
-            lax.fori_loop(0, length // tile, inward, 0)
-            if k == top:
-                head_climb()
-            else:
-                if k + 3 <= top:
-                    hand(k + 3)
-                if k + 2 <= top:
-                    level(k + 2)
-                spread(k + 1)
-                if k == top - 2:
-                    head_level()
+
+            for i in range(length // tile):
+                inward(i)
+                tick()
             for copy in bring[k][1]:
                 copy.wait()
 
-            def outward(i, carry, k=k, by=by, slot=slot, above=above):
-                place = pl.multiple_of(i * tile, 16)
+            def outward(i, k=k, by=by, slot=slot, above=above):
+                place = i * tile
                 there = hidden[slot][pl.ds(place, tile), :]
                 value = None
                 for j in range(3):
-                    piece = pull[pl.ds(pl.multiple_of(most + place + (1 - j) * by, 16), tile), :]
+                    piece = pull[pl.ds(most + place + (1 - j) * by, tile), :]
                     span = pl.ds(j * inner, inner)
                     sums[k, span, :] += contract_rows(piece, there)
                     if k:
@@ -610,25 +656,15 @@
                     value = value * slope[slot][pl.ds(place, tile), :].astype(f32)
                     value = value + above[pl.ds(place, tile), :].astype(f32)
                     grad[pl.ds(place, tile), :] = value.astype(bf16)
-                return carry
-
-            lax.fori_loop(0, length // tile, outward, 0)
-            swap(k)
-            if k + 1 <= top:
-                climb(k + 1)
-            if k + 2 <= top:
-                deliver(k + 2)
-
-        spread(0)
-        level(1)
-        hand(2)
-        climb(0)
-        deliver(1)
-        level(0)
-        hand(1)
-        deliver(0)
-        head_hand()
-        hand(0)
+
+            for i in range(length // tile):
+                outward(i)
+                tick()
+
+        while any(stages.values()):
+            for name in [*reversed(range(1, sections)), "h", 0]:
+                if stages[name]:
+                    stages[name].pop(0)()
         for copy in flight["r"]:
             copy.wait_recv()
         for k in range(sections):
@@ -663,27 +699,56 @@
             pltpu.VMEM((sections, sections - 1, quarter, channels), bf16),
             pltpu.VMEM((sections, sections - 1, quarter, channels), bf16),
             pltpu.VMEM((sections, quarter, channels), f32),
-            pltpu.VMEM((sections, zones - 1, strip, channels), f32),
+            pltpu.VMEM((sections, quarter, channels), f32),
             pltpu.VMEM((sections, quarter, channels), f32),
             pltpu.VMEM((side, tracks), f32),
             pltpu.VMEM((side, tracks), f32),
-            pltpu.VMEM((zones - 1, band, tracks), f32),
+            pltpu.VMEM((side, tracks), f32),
         ]
         + pair(sections)
         + pair(sections * (sections - 1))
-        + pair(sections * (zones - 1))
-        + pair(sections * (zones - 1))
+        + pair(sections * levels)
+        + pair(sections * levels)
         + [dma((sections,)), dma((sections,))]
         + pair(sections)
         + pair(1)
-        + pair(zones - 1)
-        + pair(zones - 1)
-        + pair(zones),
+        + pair(levels)
+        + pair(levels)
+        + pair(levels + 1),
         compiler_params=pltpu.CompilerParams(
             collective_id=2, has_side_effects=True, vmem_limit_bytes=56 * 2**20
         ),
         name="backward_tower",
     )(head_part, cot, weights, *hidden, *slope, *active, *bend)
+
+
+def finish(total, head_sum, split):
+    def kernel(total_ref, head_ref, conv_out, proj_out, head_out, sems):
+        copies = [
+            pltpu.make_async_copy(total_ref.at[pl.ds(0, split)], conv_out, sems.at[0]),
+            pltpu.make_async_copy(
+                total_ref.at[pl.ds(split, total.shape[0] - split)], proj_out, sems.at[1]
+            ),
+            pltpu.make_async_copy(head_ref, head_out, sems.at[2]),
+        ]
+        for copy in copies:
+            copy.start()
+        for copy in copies:
+            copy.wait()
+
+    width = total.shape[1]
+    return pl.pallas_call(
+        kernel,
+        out_shape=[
+            jax.ShapeDtypeStruct((split, width), total.dtype),
+            jax.ShapeDtypeStruct((total.shape[0] - split, width), total.dtype),
+            jax.ShapeDtypeStruct(head_sum.shape, head_sum.dtype),
+        ],
+        in_specs=[ANY] * 2,
+        out_specs=[ANY] * 3,
+        scratch_shapes=[pltpu.SemaphoreType.DMA((3,))],
+        name="finish",
+    )(total, head_sum)
 
 
 def plain_body(bases, targets, stem_weight, conv_weight, proj_weight, head_weight):
@@ -791,8 +856,9 @@
     total, head_sum = backward_tower(
         head_part, cot, weights, hidden, slope, active, bend, sections, zones, unit
     )
-    conv_sum = total[: 3 * inner].reshape(3, inner, channels).transpose(0, 2, 1)
-    return conv_sum[None], total[3 * inner :][None], head_sum
+    conv_sum, proj_sum, head_sum = finish(total, head_sum, 3 * inner)
+    conv_sum = conv_sum.reshape(3, inner, channels).transpose(0, 2, 1)
+    return conv_sum[None], proj_sum[None], head_sum
 
 
 def body(bases, targets, stem_weight, conv_weight, proj_weight, head_weight):
@@ -804,6 +870,7 @@
     paired = paired and unit % 16 == 0 and half % 16 == 0 and inner % 16 == 0
     paired = paired and (2 * inner) % (16 * sections) == 0
     paired = paired and (2 * inner) % (8 * sections * zones) == 0
+    paired = paired and zones & (zones - 1) == 0
     paired = paired and stem_weight.shape[1] % (16 * zones) == 0
     run = paired_body if paired else plain_body
     return run(bases, targets, stem_weight, conv_weight, proj_weight, head_weight)

time: 164 us -> 247 us (1.51)
  Pallas kernels: 154 us -> 240 us
  local copies, waits for them, and re-layouts: 9.5 us -> 4.41 us
    pallas_call x0 -> x1, Pallas kernels: none -> 84.5 us  [finish(): pl.pallas_call(kernel, out_shape=[jax.ShapeDtypeStruct((split, width), to...]
where the time goes in v3:
time: 247 us; the launch traced here: 245 us
  Pallas kernels  240 us (97%)
  local copies, waits for them, and re-layouts  4.41 us (2%)
    pallas_call x1, Pallas kernels, backward_tower(): pl.pallas_call(kernel, out_shape=[jax.ShapeDtypeStruct((rows, channels),...  89.4 us
    pallas_call x1, Pallas kernels, finish(): pl.pallas_call(kernel, out_shape=[jax.ShapeDtypeStruct((split, width), to...  84.5 us
    pallas_call x1, Pallas kernels, forward_tower(): pl.pallas_call(kernel, out_shape=[jax.ShapeDtypeStruct((seqs, half, chann...  52.3 us
    pallas_call x1, Pallas kernels, head(): pl.pallas_call(kernel, out_shape=[jax.ShapeDtypeStruct((channels, tracks)...  13.9 us

profile of v3, /device:TPU:0, one launch (start us, length us, event | category | flops | bytes accessed | tf_op | source)
XLA Modules:
  0.0 245.4 jit_solution(17881590318305014533)
XLA Ops:
  0.6 1.1 reshape.21
  1.7 0.0 copy-start.2
  1.7 0.8 copy.9
  2.5 52.3 %forward_tower.1 = (bf16[2,1536,384]{2,1,0:T(8,128)(2,1)}, bf16[4,768,384]{2,1,0:T(8,128)(2,1)}, bf16[3072,384]{1,0:T(8,128)(2,1)}, bf16[3072,384]{1,0:T(8,128)(...) custom-call(s32[2,1536,128]{2,1,0:T(8,128)} %refs_0_.1, ...), custom_call_target="tpu_custom_call" | custom-call | tf_op jit(solution)/shard_map/forward_tower/pallas_call | solution.py:258
  54.9 0.0 copy-done.2
  54.9 13.9 %head.1 = (f32[384,1024]{1,0:T(8,128)S(1)}, bf16[2,1536,384]{2,1,0:T(8,128)(2,1)S(1)}) custom-call(bf16[2,1536,384]{2,1,0:T(8,128)(2,1)} %get-tuple-element.27.top_ref, s32[2,1536,1024]{2,1,0:T(8,128)} %targets_ref.1, bf16[384,1024]{1,0:T(8,128)(2,1)S(1)} %copy-done.2), custom_call_target="tpu_custom_call" | custom-call | tf_op jit(solution)/shard_map/head/pallas_call | solution.py:349
  68.8 0.0 copy-start
  68.8 1.4 copy-done
  70.2 0.0 copy-start.1
  70.2 1.1 copy-done.1
  71.4 89.4 %backward_tower.1 = (f32[768,384]{1,0:T(8,128)}, f32[384,1024]{1,0:T(8,128)}) custom-call(f32[384,1024]{1,0:T(8,128)} %copy-done.1, bf16[3072,384]{1,0:T(8,128)(2,1)} %bitcast.16, bf16[4,768,384]{2,1,0:T(8,128)(2,1)} %get-tuple-element.30.refs_2_, bf16[3072,384]{1,0:T(8,128)(2,1)} %get-tuple-element.31.refs_3_, bf16[3072,384]{1,0:T(8,128)(2,1)} %get-tuple-element.32.refs_4_, ...), custom_call_target="tpu_custom_call" | custom-call | tf_op jit(solution)/shard_map/backward_tower/pallas_call | solution.py:682
  160.8 84.5 %finish.1 = (f32[576,384]{1,0:T(8,128)}, f32[192,384]{1,0:T(8,128)}, f32[384,1024]{1,0:T(8,128)}) custom-call(f32[768,384]{1,0:T(8,128)} %get-tuple-element.46.total_ref, f32[384,1024]{1,0:T(8,128)} %get-tuple-element.47.head_ref), custom_call_target="tpu_custom_call" | custom-call | tf_op jit(solution)/shard_map/finish/pallas_call | solution.py:740
Async XLA Ops:
  1.7 53.2 %copy-start.2 = (bf16[384,1024]{1,0:T(8,128)(2,1)S(1)}, bf16[384,1024]{1,0:T(8,128)(2,1)}, u32[]{:S(2)}) copy-start(bf16[384,1024]{1,0:T(8,128)(2,1)} %weight_ref.1) | copy-start | bytes 2359300
  68.8 1.4 copy-start
  70.2 1.1 copy-start.1
